TPU v7x, 32 devices: a whole 2x2x4 slice. The times are simulated.
32 devices in a mesh: rep: 2 (over x), fsdp: 16 (over z, y, core).
Axes of the slice: x: 2, y: 2, z: 4, core: 2. Of those that a mesh axis runs over, the one named last changes fastest.
Arguments:
- tokens: bfloat16 [512, 4096], P(('rep', 'fsdp')), may hold values from -6 to 6
- upstream: bfloat16 [512, 14336], P(('rep', 'fsdp')), may hold values from -6 to 6
- blocks: bfloat16 [224, 16, 128, 128], P('fsdp'), may hold values from -0.125 to 0.125
- keep_mask: int32 [32, 112], replicated, may hold values from 0 to 1, as said below
- panel_owner: int32 [112], replicated, may hold values from 0 to 15, as said below
Outputs:
- activation: bfloat16 [512, 14336], P(('rep', 'fsdp'))
- input_grad: bfloat16 [512, 4096], P(('rep', 'fsdp'))
- block_grad: bfloat16 [224, 16, 128, 128], P('fsdp')
Inputs may be any that keep to these rules, and one draw needn't show every extreme that they name: `keep_mask`: every column panel keeps exactly 16 of its 32 blocks. `panel_owner`: non-decreasing over the panels; a shard owns at most 14 panels, some shard owns exactly 14, and some shard owns none.
All inputs are finite; a program needn't handle non-finite values.
Results may differ from a plain program's by a relative error of at most 0.005.
Values may be sent and summed in bfloat16 or wider, within the bound.
A program may use at most 128 MiB of HBM per device.

v0:
```python
import math

import jax
import jax.numpy as jnp
from jax import lax
from jax.sharding import PartitionSpec as P


def per_device(tokens, upstream, blocks, keep_mask, panel_owner):
    shard_count = lax.axis_size("fsdp")
    own_index = lax.axis_index("fsdp")
    tok_dev = tokens.shape[0]
    model_width = tokens.shape[1]
    slot_count = blocks.shape[0]
    keep_count = blocks.shape[1]
    block_size = blocks.shape[3]
    row_blocks = keep_mask.shape[0]
    panel_count = panel_owner.shape[0]
    group_rows = tok_dev * shard_count
    shard_ids = jnp.arange(shard_count, dtype=jnp.int32)
    member = (panel_owner[:, None] == shard_ids[None, :]).astype(jnp.int32)
    counts = jnp.sum(member, axis=0)
    first_panel = jnp.cumsum(counts) - counts
    slot_ids = jnp.arange(slot_count, dtype=jnp.int32)
    panel_table = jnp.clip(first_panel[:, None] + slot_ids[None, :], 0, panel_count - 1)
    is_mine = shard_ids == own_index
    own_first = jnp.sum(jnp.where(is_mine, first_panel, 0))
    own_count = jnp.sum(jnp.where(is_mine, counts, 0))
    own_live = slot_ids < own_count
    own_panels = jnp.clip(own_first + slot_ids, 0, panel_count - 1)
    panel_ids = jnp.arange(panel_count, dtype=jnp.int32)
    panel_pick = (panel_ids[None, :] == own_panels[:, None]).astype(jnp.int32)
    running = jnp.cumsum(keep_mask, axis=0)
    own_running = jnp.sum(panel_pick[:, None, :] * running[None, :, :], axis=2)
    pick_ids = jnp.arange(keep_count, dtype=jnp.int32)
    own_rows = jnp.sum(
        (own_running[:, :, None] <= pick_ids[None, None, :]).astype(jnp.int32), axis=1
    )
    upstream_panels = jnp.transpose(upstream.reshape(tok_dev, panel_count, block_size), (1, 0, 2))
    outgoing = jnp.take(upstream_panels, panel_table.reshape(-1), axis=0)
    incoming = lax.all_to_all(outgoing, "fsdp", split_axis=0, concat_axis=1, tiled=True)
    group_tokens = lax.all_gather(tokens, "fsdp", axis=0, tiled=True)
    token_blocks = group_tokens.reshape(group_rows, row_blocks, block_size)

    def panel_step(nothing, panel_item):
        row_ids, weights, cotangent, is_live = panel_item
        chosen = jnp.take(token_blocks, row_ids, axis=1).reshape(
            group_rows, keep_count * block_size
        )
        flat_weights = weights.reshape(keep_count * block_size, block_size)
        preact = jnp.dot(chosen, flat_weights, preferred_element_type=jnp.float32)
        activation = jax.nn.silu(preact).astype(jnp.bfloat16)
        sigmoid_z = jax.nn.sigmoid(preact)
        slope = sigmoid_z * (1.0 + preact * (1.0 - sigmoid_z))
        dpre = jnp.where(is_live, cotangent.astype(jnp.float32) * slope, 0.0).astype(jnp.bfloat16)
        weight_grad = lax.dot_general(
            chosen, dpre, (((0,), (0,)), ((), ())), preferred_element_type=jnp.float32
        )
        return (
            nothing,
            (activation, weight_grad.reshape(keep_count, block_size, block_size), dpre),
        )

    panel_items = (own_rows, blocks, incoming, own_live)
    nothing, (activations, weight_grads, dpres) = lax.scan(
        panel_step, jnp.zeros((), jnp.float32), panel_items
    )
    dense_panels = jnp.zeros((slot_count, row_blocks, block_size, block_size), blocks.dtype)
    dense_panels = dense_panels.at[slot_ids[:, None], own_rows].set(blocks)
    backward = lax.dot_general(
        dpres, dense_panels, (((0, 2), (0, 3)), ((), ())), preferred_element_type=jnp.float32
    )
    input_grad = lax.psum_scatter(
        backward.reshape(dpres.shape[1], model_width), "fsdp", scatter_dimension=0, tiled=True
    ).astype(jnp.bfloat16)
    returned = lax.all_to_all(activations, "fsdp", split_axis=1, concat_axis=0, tiled=True)
    panel_first = jnp.sum(member * first_panel[None, :], axis=1)
    panel_slot = panel_owner * slot_count + panel_ids - panel_first
    act_panels = jnp.take(returned, panel_slot, axis=0)
    activation_out = jnp.transpose(act_panels, (1, 0, 2)).reshape(tok_dev, panel_count * block_size)
    scale = 1.0 / math.sqrt(group_rows * lax.axis_size("rep"))
    summed = lax.psum(weight_grads, "rep")
    block_grad = (summed * scale).astype(jnp.bfloat16)
    return (activation_out, input_grad, block_grad)


def solution(mesh):
    return jax.shard_map(
        per_device,
        mesh=mesh,
        in_specs=(
            P(("rep", "fsdp"), None),
            P(("rep", "fsdp"), None),
            P("fsdp", None, None, None),
            P(),
            P(),
        ),
        out_specs=(P(("rep", "fsdp"), None), P(("rep", "fsdp"), None), P("fsdp", None, None, None)),
        check_vma=False,
    )
```

profile of v0, /device:TPU:0, one launch (start us, length us, event | category | flops | bytes accessed | tf_op | source)
XLA Modules:
  0.0 683.9 jit_solution(11434107155219321135)
XLA Ops:
  12.0 7.4 %all-to-all-start = ((bf16[224,16,128]{2,1,0:T(8,128)(2,1)}), bf16[224,16,128]{2,1,0:T(8,128)(2,1)S(1)}, u32[]{:S(2)}, u32[]{:S(2)}) async-start(bf16[224,16,128]{2,1,0:T(8,128)(2,1)} %broadcast_select_fusion.1), calls=%async_computation | async-start | bytes 1835008 | tf_op jit(solution)/shard_map/all_to_all | solution.py:41
  21.7 8.9 %broadcast_in_dim.89 = bf16[14,32,128,128]{3,2,1,0:T(8,128)(2,1)} broadcast(bf16[]{:T(256)} %constant.87.clone.1), dimensions={} | broadcast | bytes 14680066 | tf_op jit(solution)/shard_map/broadcast_in_dim | solution.py:68
  30.7 36.0 %scatter_fusion = bf16[14,32,128,128]{3,2,1,0:T(8,128)(2,1)} fusion(bf16[14,32,128,128]{3,2,1,0:T(8,128)(2,1)} %broadcast_in_dim.89, s32[224]{0:T(256)S(1)} %reshape.254, bf16[224,128,128]{2,1,0:T(8,128)(2,1)} %bitcast.124), kind=kCustom, calls=%fused_computation.3 | custom fusion | bytes 22021888 | tf_op jit(solution)/shard_map/scatter | solution.py:69
  67.5 3.3 copy.41
  70.8 2.9 copy.44
  73.6 166.1 %while.14 = (s32[]{:T(128)}, bf16[14,256,128]{2,1,0:T(8,128)(2,1)}, f32[14,16,128,128]{3,2,1,0:T(8,128)}, bf16[14,256,128]{2,1,0:T(8,128)(2,1)}, s32[14,16]{1,0:...) while((s32[]{:T(128)}, bf16[14,256,128]{2,1,0:T(8,128)(2,1)}, ...), condition=%wide.region_9.10_spmd, body=%wide.region_8.9_spmd.sunk | while | flops 270271616 | bytes 15739879 | solution.py:65
  73.7 2.3 gather_fusion
  79.2 3.0 bitcast_dynamic-update-slice_fusion.3
  83.4 2.1 fusion.31
  85.5 2.3 gather_fusion
  91.1 3.0 bitcast_dynamic-update-slice_fusion.3
  95.2 2.1 fusion.31
  97.4 2.3 gather_fusion
  103.0 3.0 bitcast_dynamic-update-slice_fusion.3
  109.3 2.3 gather_fusion
  114.8 3.0 bitcast_dynamic-update-slice_fusion.3
  119.0 2.1 fusion.31
  121.1 2.3 gather_fusion
  126.7 3.0 bitcast_dynamic-update-slice_fusion.3
  133.0 2.3 gather_fusion
  138.5 3.0 bitcast_dynamic-update-slice_fusion.3
  142.7 2.1 fusion.31
  144.9 2.3 gather_fusion
  150.4 3.0 bitcast_dynamic-update-slice_fusion.3
  154.6 2.1 fusion.31
  156.7 2.3 gather_fusion
  162.3 3.0 bitcast_dynamic-update-slice_fusion.3
  168.6 2.3 gather_fusion
  174.1 3.0 bitcast_dynamic-update-slice_fusion.3
  178.3 2.2 fusion.31
  180.5 2.3 gather_fusion
  186.1 3.0 bitcast_dynamic-update-slice_fusion.3
  192.3 2.3 gather_fusion
  197.9 3.0 bitcast_dynamic-update-slice_fusion.3
  204.2 2.3 gather_fusion
  209.8 3.0 bitcast_dynamic-update-slice_fusion.3
  216.0 2.3 gather_fusion
  221.6 3.0 bitcast_dynamic-update-slice_fusion.3
  225.8 2.2 fusion.31
  227.9 2.3 gather_fusion
  233.5 3.0 bitcast_dynamic-update-slice_fusion.3
  239.7 11.5 %fusion.6 = f32[256,32,128,1]{0,2,1,3:T(8,128)} fusion(bf16[14,32,128,128]{3,2,1,0:T(8,128)(2,1)} %scatter_fusion, bf16[14,256,128]{2,1,0:T(8,128)(2,1)} %get-tuple-element.53), kind=kOutput, calls=%fused_computation.25 | convolution fusion | flops 3758096384 | bytes 19791872 | tf_op jit(solution)/shard_map/dot_general | solution.py:70
  251.3 5.7 copy.50
  259.3 6.0 all-to-all-start.1
  265.4 22.8 %all-to-all-done.1 = bf16[14,256,128]{2,0,1:T(8,128)(2,1)S(1)} async-done(((bf16[14,256,128]{2,0,1:T(8,128)(2,1)}), bf16[14,256,128]{2,0,1:T(8,128)(2,1)S(1)}, u32[]{:S(2)}, u32[]{:S(2)}) %all-to-all-start.1) | async-done | bytes 917536 | tf_op jit(solution)/shard_map/all_to_all | solution.py:76
  290.1 41.9 %reduce-scatter.2.cloned.1.call-done = f32[16,4096]{1,0:T(8,128)} async-done(((f32[256,4096]{1,0:T(8,128)}), f32[16,4096]{1,0:T(8,128)}) %reduce-scatter.2.cloned.1.call-update) | async-done | bytes 262160 | tf_op jit(solution)/shard_map/reduce_scatter | solution.py:73
  333.7 333.3 %all-reduce.2.cloned.1.call-done = f32[14,16,128,128]{3,2,1,0:T(8,128)} async-done(((f32[14,16,128,128]{3,2,1,0:T(8,128)}), f32[14,16,128,128]{3,2,1,0:T(8,128)}) %all-reduce.2.cloned.1.call-update) | async-done | bytes 14680080 | tf_op jit(solution)/shard_map/psum | solution.py:82
  666.9 10.4 %multiply_convert_fusion.1 = bf16[14,16,128,128]{3,2,1,0:T(8,128)(2,1)} fusion(f32[14,16,128,128]{3,2,1,0:T(8,128)} %all-reduce.2.cloned.1.call-done), kind=kLoop, calls=%fused_computation.24 | loop fusion | flops 7340032 | bytes 22020096 | tf_op jit(solution)/shard_map/convert_element_type | solution.py:83
  (197 shorter events, 89.2 us)
Async XLA Ops:
  7.2 2.7 copy-start
  7.2 60.3 %all-gather.2.cloned.1.call-start = ((), (), s32[]{:S(2)}) async-start(), calls=%async_computation.3 | async-start | bytes 2228224 | tf_op jit(solution)/shard_map/all_gather | solution.py:42
  12.0 55.2 %all-to-all-start = ((bf16[224,16,128]{2,1,0:T(8,128)(2,1)}), bf16[224,16,128]{2,1,0:T(8,128)(2,1)S(1)}, u32[]{:S(2)}, u32[]{:S(2)}) async-start(bf16[224,16,128]{2,1,0:T(8,128)(2,1)} %broadcast_select_fusion.1), calls=%async_computation | async-start | bytes 1835008 | tf_op jit(solution)/shard_map/all_to_all | solution.py:41
  19.4 312.6 %reduce-scatter.2.cloned.1.call-start = ((), (), s32[]{:S(2)}) async-start(), calls=%async_computation.4 | async-start | bytes 4456448 | tf_op jit(solution)/shard_map/reduce_scatter | solution.py:73
  251.3 6.5 copy-start.2
  251.3 14.0 %copy-start.3 = (s32[112]{0:T(128)S(1)}, s32[112]{0:T(128)}, u32[]{:S(2)}) copy-start(s32[112]{0:T(128)} %param.11) | copy-start | bytes 1348
  257.0 410.0 %all-reduce.2.cloned.1.call-start = ((), (), s32[]{:S(2)}) async-start(), calls=%async_computation.5 | async-start | bytes 29360128 | tf_op jit(solution)/shard_map/psum | solution.py:82
  257.7 419.6 %copy-start.1 = (bf16[16,14336]{1,0:T(8,128)(2,1)S(1)}, bf16[16,14336]{1,0:T(8,128)(2,1)}, u32[]{:S(2)}) copy-start(bf16[16,14336]{1,0:T(8,128)(2,1)} %param.8) | copy-start | bytes 1376260
  259.3 28.9 %all-to-all-start.1 = ((bf16[14,256,128]{2,0,1:T(8,128)(2,1)}), bf16[14,256,128]{2,0,1:T(8,128)(2,1)S(1)}, u32[]{:S(2)}, u32[]{:S(2)}) async-start(bf16[14,256,128]{2,0,1:T(8,128)(2,1)} %copy.45), calls=%async_computation.1 | async-start | bytes 2097152 | tf_op jit(solution)/shard_map/all_to_all | solution.py:76
Sparse Core Ops, SparseCore 0:
  10.2 52.8 all-gather.1
  257.1 74.8 reduce-scatter.1
  334.7 332.2 all-reduce.1
where the time goes:
time: 687 us; the launch traced here: 684 us
  waiting for transfers between devices  399 us (58%)
  local copies, waits for them, and re-layouts  144 us (21%)
  matrix products  83.4 us (12%)
  other arithmetic  28.7 us (4%)
  between operations  13.9 us (2%)
  starting transfers between devices  13.7 us (2%)
    psum x1, waiting for transfers between devices, per_device(): summed = lax.psum(weight_grads, 'rep')  333 us
    dot_general x14, matrix products, panel_step(): preact = jnp.dot(chosen, flat_weights, preferred_element_type=jnp.float32)  42.4 us
    reduce_scatter x1, waiting for transfers between devices, per_device(): lax.psum_scatter(backward.reshape(dpres.shape[1], model_width), 'fsdp', s...  41.9 us
    gather x28, local copies, waits for them, and re-layouts, panel_step(): jnp.take(token_blocks, row_ids, axis=1)  40.1 us
    scatter x1, local copies, waits for them, and re-layouts, per_device(): dense_panels = dense_panels.at[slot_ids[:, None], own_rows].set(blocks)  36 us
    dot_general x14, matrix products, panel_step(): lax.dot_general(chosen, dpre, (((0,), (0,)), ((), ())), preferred_element...  29.5 us
    dynamic_slice x28, local copies, waits for them, and re-layouts, per_device(): lax.scan(panel_step, jnp.zeros((), jnp.float32), panel_items)  23.2 us
    all_to_all x1, waiting for transfers between devices, per_device(): lax.all_to_all(activations, 'fsdp', split_axis=1, concat_axis=0, tiled=True)  22.8 us
  transfers between devices with their start and end apart: 5, of which 3 were waited for; matrix products, arithmetic and copies ran while one was open for 8% of the time, Pallas kernels for 0%

commit v1 on v0

v1 whole, which is shorter than its diff:
```python
import functools
import math

import jax
import jax.numpy as jnp
from jax import lax
from jax.experimental import pallas as pl
from jax.experimental.pallas import tpu as pltpu
from jax.sharding import PartitionSpec as P

BF16 = jnp.bfloat16
F32 = jnp.float32
MESH = pl.DeviceIdType.MESH
VMEM_LIMIT = 60 * 1024 * 1024
NZ, NY, NC = 4, 2, 2
NF = NZ * NY * NC


def per_device_general(tokens, upstream, blocks, keep_mask, panel_owner):
    shard_count = lax.axis_size("fsdp")
    own_index = lax.axis_index("fsdp")
    tok_dev = tokens.shape[0]
    model_width = tokens.shape[1]
    slot_count = blocks.shape[0]
    keep_count = blocks.shape[1]
    block_size = blocks.shape[3]
    row_blocks = keep_mask.shape[0]
    panel_count = panel_owner.shape[0]
    group_rows = tok_dev * shard_count
    rep_count = lax.axis_size("rep")
    shard_ids = jnp.arange(shard_count, dtype=jnp.int32)
    member = (panel_owner[:, None] == shard_ids[None, :]).astype(jnp.int32)
    counts = jnp.sum(member, axis=0)
    first_panel = jnp.cumsum(counts) - counts
    slot_ids = jnp.arange(slot_count, dtype=jnp.int32)
    panel_table = jnp.clip(first_panel[:, None] + slot_ids[None, :], 0, panel_count - 1)
    is_mine = shard_ids == own_index
    own_first = jnp.sum(jnp.where(is_mine, first_panel, 0))
    own_count = jnp.sum(jnp.where(is_mine, counts, 0))
    own_live = slot_ids < own_count
    own_panels = jnp.clip(own_first + slot_ids, 0, panel_count - 1)
    panel_ids = jnp.arange(panel_count, dtype=jnp.int32)
    panel_pick = (panel_ids[None, :] == own_panels[:, None]).astype(jnp.int32)
    running = jnp.cumsum(keep_mask, axis=0)
    own_running = jnp.sum(panel_pick[:, None, :] * running[None, :, :], axis=2)
    pick_ids = jnp.arange(keep_count, dtype=jnp.int32)
    own_rows = jnp.sum(
        (own_running[:, :, None] <= pick_ids[None, None, :]).astype(jnp.int32), axis=1
    )
    upstream_panels = jnp.transpose(upstream.reshape(tok_dev, panel_count, block_size), (1, 0, 2))
    outgoing = jnp.take(upstream_panels, panel_table.reshape(-1), axis=0)
    incoming = lax.all_to_all(outgoing, "fsdp", split_axis=0, concat_axis=1, tiled=True)
    group_tokens = lax.all_gather(tokens, "fsdp", axis=0, tiled=True)
    all_tokens = lax.all_gather(group_tokens, "rep", axis=0, tiled=True)
    token_blocks = jnp.transpose(all_tokens).reshape(row_blocks, block_size, rep_count * group_rows)

    dense_panels = jnp.zeros((slot_count, row_blocks, block_size, block_size), blocks.dtype)
    dense_panels = dense_panels.at[slot_ids[:, None], own_rows].set(blocks)
    dense = dense_panels.reshape(slot_count, model_width, block_size)
    preact = lax.dot_general(
        group_tokens, dense, (((1,), (1,)), ((), ())), preferred_element_type=jnp.float32
    )
    sigmoid_z = jax.nn.sigmoid(preact)
    activations = (preact * sigmoid_z).astype(jnp.bfloat16)
    slope = sigmoid_z * (1.0 + preact * (1.0 - sigmoid_z))
    cot = jnp.transpose(incoming, (1, 0, 2)).astype(jnp.float32)
    dpre = jnp.where(own_live[None, :, None], cot * slope, 0.0).astype(jnp.bfloat16)
    dpre_all = lax.all_gather(dpre, "rep", axis=0, tiled=True)
    backward = lax.dot_general(
        dpre, dense, (((1, 2), (0, 2)), ((), ())), preferred_element_type=jnp.float32
    )
    input_grad = lax.psum_scatter(
        backward, "fsdp", scatter_dimension=0, tiled=True
    ).astype(jnp.bfloat16)
    returned = lax.all_to_all(activations, "fsdp", split_axis=0, concat_axis=1, tiled=True)
    panel_first = jnp.sum(member * first_panel[None, :], axis=1)
    panel_slot = panel_owner * slot_count + panel_ids - panel_first
    act_panels = jnp.take(returned, panel_slot, axis=1)
    activation_out = act_panels.reshape(tok_dev, panel_count * block_size)
    scale = 1.0 / math.sqrt(group_rows * rep_count)

    def panel_step(nothing, item):
        row_ids, dz = item
        chosen = jnp.take(token_blocks, row_ids, axis=0)
        grad = lax.dot_general(
            chosen, dz, (((2,), (0,)), ((), ())), preferred_element_type=jnp.float32
        )
        return nothing, (grad * scale).astype(jnp.bfloat16)

    nothing, block_grad = lax.scan(
        panel_step, jnp.zeros((), jnp.float32), (own_rows, jnp.transpose(dpre_all, (1, 0, 2)))
    )
    return (activation_out, input_grad, block_grad)


class Place:
    def __init__(self):
        self.rep = lax.axis_index("rep")
        self.me = lax.axis_index("fsdp")
        self.core = self.me % NC
        self.y = (self.me // NC) % NY
        self.z = self.me // (NC * NY)

    def at(self, z, y, core):
        return (z * NY + y) * NC + core

    def z_back(self, step):
        return (self.z + NZ - step) % NZ

    def z_ahead(self, step):
        return (self.z + step) % NZ

    def fsdp_peer(self, step):
        return (self.me + step) % NF

    def greet(self):
        barrier = pltpu.get_barrier_semaphore()
        for step in range(1, NF):
            pl.semaphore_signal(
                barrier, inc=1, device_id=(self.rep, self.fsdp_peer(step)), device_id_type=MESH
            )
        pl.semaphore_signal(barrier, inc=1, device_id=(1 - self.rep, self.me), device_id_type=MESH)
        pl.semaphore_wait(barrier, NF)


def send(src, dst, sems, slot, device):
    send_sems, recv_sems = sems
    copy = pltpu.make_async_remote_copy(
        src_ref=src,
        dst_ref=dst,
        send_sem=send_sems.at[slot],
        recv_sem=recv_sems.at[slot],
        device_id=device,
        device_id_type=MESH,
    )
    copy.start()
    return copy


def pick_kernel(table, upstream, outgoing):
    slots, bs = outgoing.shape[1], outgoing.shape[3]

    @pl.loop(0, outgoing.shape[0])
    def _(k):
        for p in range(slots):
            column = pl.multiple_of(table[k * slots + p] * bs, bs)
            outgoing[k, p] = upstream[:, pl.ds(column, bs)]


def gather_kernel(
    tokens, outgoing, all_tokens, incoming,
    z_s, z_r, y_s, y_r, x_s, x_r, d_s, d_r, c_s, c_r, u_s, u_r,
):
    place = Place()
    rep, me, z, y, core = place.rep, place.me, place.z, place.y, place.core
    y_peer = (rep, place.at(z, 1 - y, core))
    x_peer = (1 - rep, me)
    core_peer = (rep, place.at(z, y, 1 - core))
    z_sems, y_sems, x_sems = (z_s, z_r), (y_s, y_r), (x_s, x_r)
    d_sems, c_sems, u_sems = (d_s, d_r), (c_s, c_r), (u_s, u_r)

    all_tokens[rep, me] = tokens[...]
    place.greet()
    pending = []
    own = all_tokens.at[rep, me]
    z_copies = {}
    for step in range(1, NZ):
        peer = (rep, place.at(place.z_ahead(step), y, core))
        z_copies[step] = send(own, own, z_sems, step - 1, peer)
    pending += list(z_copies.values())
    y_copies, x_copies, d_copies, c_copies = [], [], [None] * NZ, []

    def spread(step):
        piece = all_tokens.at[rep, place.at(place.z_back(step), y, core)]
        x_copies.append(send(piece, piece, x_sems, step, x_peer))
        y_copies.append(send(piece, piece, y_sems, step, y_peer))
        c_copies.append(send(piece, piece, c_sems, step, core_peer))

    spread(0)

    incoming[me] = outgoing[me]
    u_copies = []
    for step in range(1, NF):
        peer = place.fsdp_peer(step)
        u_copies.append(
            send(outgoing.at[peer], incoming.at[me], u_sems, step - 1, (rep, peer))
        )
    for step in range(1, NZ):
        z_copies[step].wait_recv()
        spread(step)
    for step in range(NZ):
        f_x = place.at(place.z_back(step), y, core)
        f_y = place.at(place.z_back(step), 1 - y, core)
        x_copies[step].wait_recv()
        piece = all_tokens.at[1 - rep, f_x]
        if step % 2 == 0:
            d_copies[step] = send(piece, piece, d_sems, step, y_peer)
        c_copies.append(send(piece, piece, c_sems, NZ + step, core_peer))
        y_copies[step].wait_recv()
        piece = all_tokens.at[rep, f_y]
        if step % 2 == 1:
            d_copies[step] = send(piece, piece, d_sems, step, x_peer)
        c_copies.append(send(piece, piece, c_sems, 2 * NZ + step, core_peer))
    for step in range(NZ):
        d_copies[step].wait_recv()
        piece = all_tokens.at[1 - rep, place.at(place.z_back(step), 1 - y, core)]
        c_copies.append(send(piece, piece, c_sems, 3 * NZ + step, core_peer))
    for copy in c_copies:
        copy.wait_recv()
    for copy in u_copies:
        copy.wait_recv()
    for copy in pending + y_copies + x_copies + d_copies + c_copies + u_copies:
        copy.wait_send()


def forward_kernel(
    info, tokens, blocks, cotangent, act, dz, part, dense, dz_all
):
    pair = pl.program_id(0)
    pairs = pl.num_programs(0)
    keep, bs = blocks.shape[1], blocks.shape[2]
    rows = tokens.shape[1] * tokens.shape[2]
    width = tokens.shape[3]
    lanes = pl.ds(pl.multiple_of(pair * 2 * bs, 2 * bs), 2 * bs)
    dense[:, lanes] = jnp.zeros((width, 2 * bs), BF16)
    for side in range(2):
        side_lanes = pl.ds(pl.multiple_of(pair * 2 * bs + side * bs, bs), bs)
        for j in range(keep):
            row = info[2 + (2 * pair + side) * keep + j]
            dense[pl.ds(pl.multiple_of(row * bs, bs), bs), side_lanes] = blocks[side, j]
    preact = jnp.dot(
        tokens[0].reshape(rows, width), dense[:, lanes], preferred_element_type=F32
    )
    for side in range(2):
        zed = preact[:, side * bs:(side + 1) * bs]
        sig = jax.nn.sigmoid(zed)
        act[:, side] = (zed * sig).astype(BF16).reshape(act.shape[0], act.shape[2], bs)
        slope = sig * (1.0 + zed * (1.0 - sig))
        cot = cotangent[:, side].reshape(rows, bs).astype(F32)
        live = 2 * pair + side < info[1]
        value = jnp.where(live, cot * slope, 0.0).astype(BF16)
        dz[side] = value
        dz_all[:, pl.ds(pl.multiple_of(pair * 2 * bs + side * bs, bs), bs)] = value

    @pl.when(pair == pairs - 1)
    def _():
        chunk = 512

        @pl.loop(0, width // chunk)
        def _(n):
            span = pl.ds(pl.multiple_of(n * chunk, chunk), chunk)
            value = lax.dot_general(
                dz_all[...], dense[span, :], (((1,), (1,)), ((), ())), preferred_element_type=F32
            )
            part[:, :, span] = value.astype(BF16).reshape(part.shape[0], part.shape[1], chunk)


def scatter_kernel(
    table, dz, act, part, dz_both, act_out, grad_out,
    act_in, r1, s2, r2, s3, r3,
    x_s, x_r, a_s, a_r, s1_s, s1_r, s2_s, s2_r, s3_s, s3_r,
):
    place = Place()
    rep, me, z, y, core = place.rep, place.me, place.z, place.y, place.core
    slots = act.shape[1]
    bs = act.shape[3]
    panels = act_out.shape[1] // bs
    y_peer = (rep, place.at(z, 1 - y, core))
    core_peer = (rep, place.at(z, y, 1 - core))
    place.greet()
    sends = []
    one = []
    for turn in range(NY):
        to_y = (y + 1 + turn) % NY
        for step in range(NZ):
            to_z = place.z_ahead(step)
            one.append(send(
                part.at[place.at(to_z, to_y, 1 - core)],
                r1.at[turn * NZ + step],
                (s1_s, s1_r), turn * NZ + step, core_peer,
            ))
    x_copy = send(dz, dz_both.at[rep], (x_s, x_r), 0, (1 - rep, me))
    a_copies = []
    for step in range(1, NF):
        peer = place.fsdp_peer(step)
        a_copies.append(send(
            act.at[peer], act_in.at[pl.ds(me * slots, slots)], (a_s, a_r), step - 1, (rep, peer)
        ))
    dz_both[rep] = dz[...]
    act_in[pl.ds(me * slots, slots)] = act[me]
    two = []
    for step in range(NZ):
        one[step].wait_recv()
        f = place.at(place.z_ahead(step), 1 - y, core)
        s2[step] = (part[f].astype(F32) + r1[step].astype(F32)).astype(BF16)
        two.append(send(s2.at[step], r2.at[step], (s2_s, s2_r), step, y_peer))

    def mine(step):
        one[NZ + step].wait_recv()
        two[step].wait_recv()
        f = place.at(place.z_ahead(step), y, core)
        return part[f].astype(F32) + r1[NZ + step].astype(F32) + r2[step].astype(F32)

    three = []
    for step in range(1, NZ):
        s3[step - 1] = mine(step).astype(BF16)
        peer = (rep, place.at(place.z_ahead(step), y, core))
        three.append(send(s3.at[step - 1], r3.at[step - 1], (s3_s, s3_r), step - 1, peer))
    total = mine(0)
    for step in range(1, NZ):
        three[step - 1].wait_recv()
        total = total + r3[step - 1].astype(F32)
    grad_out[...] = total.astype(BF16)
    for copy in a_copies:
        copy.wait_recv()

    @pl.loop(0, panels)
    def _(c):
        act_out[:, pl.ds(pl.multiple_of(c * bs, bs), bs)] = act_in[table[c]]

    x_copy.wait_recv()
    for copy in one + two + three + a_copies + [x_copy]:
        copy.wait_send()


def weight_kernel(scale, info, tokens, dz, out, turned):
    pair = pl.program_id(0)
    keep, bs = out.shape[1], out.shape[2]
    rows = tokens.shape[0]
    row_blocks = turned.shape[0]

    @pl.when(pair == 0)
    def _():
        @pl.loop(0, row_blocks)
        def _(r):
            turned[r] = tokens[:, pl.ds(pl.multiple_of(r * bs, bs), bs)].T

    for side in range(out.shape[0]):
        value = dz[:, side].reshape(rows, bs)
        for j in range(keep):
            row = info[2 + (out.shape[0] * pair + side) * keep + j]
            out[side, j] = (
                jnp.dot(turned[row], value, preferred_element_type=F32) * scale
            ).astype(BF16)


def per_device(tokens, upstream, blocks, keep_mask, panel_owner):
    tok_dev, width = tokens.shape
    slots, keep, bs, _ = blocks.shape
    panels = panel_owner.shape[0]
    row_blocks = keep_mask.shape[0]
    reps = 2
    me = lax.axis_index("fsdp")
    rep = lax.axis_index("rep")
    shard_ids = jnp.arange(NF, dtype=jnp.int32)
    slot_ids = jnp.arange(slots, dtype=jnp.int32)
    panel_ids = jnp.arange(panels, dtype=jnp.int32)
    member = (panel_owner[:, None] == shard_ids[None, :]).astype(jnp.int32)
    counts = jnp.sum(member, axis=0)
    below = (panel_owner[:, None] < shard_ids[None, :]).astype(jnp.int32)
    first = jnp.sum(below, axis=0)
    send_table = jnp.clip(first[:, None] + slot_ids[None, :], 0, panels - 1).reshape(-1)
    panel_first = jnp.sum(member * first[None, :], axis=1)
    panel_slot = panel_owner * slots + panel_ids - panel_first
    is_mine = (shard_ids == me).astype(jnp.int32)
    own_first = jnp.sum(is_mine * first)
    own_count = jnp.sum(is_mine * counts)
    own_panels = jnp.clip(own_first + slot_ids, 0, panels - 1)
    pick = (panel_ids[None, :] == own_panels[:, None]).astype(jnp.int32)
    running = jnp.cumsum(keep_mask, axis=0)
    own_running = jnp.sum(pick[:, None, :] * running[None, :, :], axis=2)
    keep_ids = jnp.arange(keep, dtype=jnp.int32)
    own_rows = jnp.sum(
        (own_running[:, :, None] <= keep_ids[None, None, :]).astype(jnp.int32), axis=1
    )
    info = jnp.concatenate([jnp.stack([rep, own_count]), own_rows.reshape(-1)]).astype(jnp.int32)

    smem = pl.BlockSpec(memory_space=pltpu.SMEM)
    vmem = pl.BlockSpec(memory_space=pltpu.VMEM)
    dma = lambda n: [pltpu.SemaphoreType.DMA((n,))] * 2
    params = functools.partial(pltpu.CompilerParams, vmem_limit_bytes=VMEM_LIMIT)
    outgoing = pl.pallas_call(
        pick_kernel,
        out_shape=jax.ShapeDtypeStruct((NF, slots, tok_dev, bs), BF16),
        in_specs=[smem, vmem],
        out_specs=vmem,
        compiler_params=params(),
        name="pick_cotangents",
    )(send_table, upstream)
    all_tokens, incoming = pl.pallas_call(
        gather_kernel,
        out_shape=(
            jax.ShapeDtypeStruct((reps, NF, tok_dev, width), BF16),
            jax.ShapeDtypeStruct((NF, slots, tok_dev, bs), BF16),
        ),
        in_specs=[vmem, vmem],
        out_specs=(vmem, vmem),
        scratch_shapes=dma(NZ - 1) + dma(NZ) + dma(NZ) + dma(NZ) + dma(4 * NZ) + dma(NF - 1),
        compiler_params=params(collective_id=0, has_side_effects=True),
        name="gather_tokens",
    )(tokens, outgoing)

    group = NF * tok_dev
    act, dz, part = pl.pallas_call(
        forward_kernel,
        out_shape=(
            jax.ShapeDtypeStruct((NF, slots, tok_dev, bs), BF16),
            jax.ShapeDtypeStruct((slots, group, bs), BF16),
            jax.ShapeDtypeStruct((NF, tok_dev, width), BF16),
        ),
        grid_spec=pltpu.PrefetchScalarGridSpec(
            num_scalar_prefetch=1,
            grid=(slots // 2,),
            in_specs=[
                pl.BlockSpec((1, NF, tok_dev, width), lambda i, s: (s[0], 0, 0, 0)),
                pl.BlockSpec((2, keep, bs, bs), lambda i, s: (i, 0, 0, 0)),
                pl.BlockSpec((NF, 2, tok_dev, bs), lambda i, s: (0, i, 0, 0)),
            ],
            out_specs=[
                pl.BlockSpec((NF, 2, tok_dev, bs), lambda i, s: (0, i, 0, 0)),
                pl.BlockSpec((2, group, bs), lambda i, s: (i, 0, 0)),
                pl.BlockSpec((NF, tok_dev, width), lambda i, s: (0, 0, 0)),
            ],
            scratch_shapes=[
                pltpu.VMEM((width, slots * bs), BF16),
                pltpu.VMEM((group, slots * bs), BF16),
            ],
        ),
        compiler_params=params(),
        name="forward_panels",
    )(info, all_tokens, blocks, incoming)

    dz_both, act_out, input_grad = pl.pallas_call(
        scatter_kernel,
        out_shape=(
            jax.ShapeDtypeStruct((reps, slots, group, bs), BF16),
            jax.ShapeDtypeStruct((tok_dev, panels * bs), BF16),
            jax.ShapeDtypeStruct((tok_dev, width), BF16),
        ),
        in_specs=[smem, vmem, vmem, vmem],
        out_specs=(vmem, vmem, vmem),
        scratch_shapes=[
            pltpu.VMEM((NF * slots, tok_dev, bs), BF16),
            pltpu.VMEM((NY * NZ, tok_dev, width), BF16),
            pltpu.VMEM((NZ, tok_dev, width), BF16),
            pltpu.VMEM((NZ, tok_dev, width), BF16),
            pltpu.VMEM((NZ - 1, tok_dev, width), BF16),
            pltpu.VMEM((NZ - 1, tok_dev, width), BF16),
        ]
        + dma(1) + dma(NF - 1) + dma(NY * NZ) + dma(NZ) + dma(NZ - 1),
        compiler_params=params(collective_id=1, has_side_effects=True),
        name="scatter_results",
    )(panel_slot, dz, act, part)

    scale = 1.0 / math.sqrt(group * reps)
    block_grad = pl.pallas_call(
        functools.partial(weight_kernel, scale),
        out_shape=jax.ShapeDtypeStruct(blocks.shape, BF16),
        grid_spec=pltpu.PrefetchScalarGridSpec(
            num_scalar_prefetch=1,
            grid=(slots // 2,),
            in_specs=[
                pl.BlockSpec((reps * group, width), lambda i, s: (0, 0)),
                pl.BlockSpec((reps, 2, group, bs), lambda i, s: (0, i, 0, 0)),
            ],
            out_specs=pl.BlockSpec((2, keep, bs, bs), lambda i, s: (i, 0, 0, 0)),
            scratch_shapes=[pltpu.VMEM((row_blocks, bs, reps * group), BF16)],
        ),
        compiler_params=params(),
        name="weight_panels",
    )(info, all_tokens.reshape(reps * group, width), dz_both)
    return (act_out, input_grad, block_grad)


def solution(mesh):
    fits = mesh.shape["rep"] == 2 and mesh.shape["fsdp"] == NF
    return jax.shard_map(
        per_device if fits else per_device_general,
        mesh=mesh,
        in_specs=(
            P(("rep", "fsdp"), None),
            P(("rep", "fsdp"), None),
            P("fsdp", None, None, None),
            P(),
            P(),
        ),
        out_specs=(P(("rep", "fsdp"), None), P(("rep", "fsdp"), None), P("fsdp", None, None, None)),
        check_vma=False,
    )
```

time: 687 us -> 131 us (0.19)
  waiting for transfers between devices: 399 us -> 0 us
  local copies, waits for them, and re-layouts: 144 us -> 2.17 us
  Pallas kernels: 0 us -> 121 us
  matrix products: 83.4 us -> 0 us
  other arithmetic: 28.7 us -> 6.78 us
  starting transfers between devices: 13.7 us -> 0 us
  between operations: 13.9 us -> 0.69 us
    psum x1 -> x0, waiting for transfers between devices: 333 us -> none  [per_device(): summed = lax.psum(weight_grads, 'rep')]
    pallas_call x0 -> x5, Pallas kernels: none -> 121 us  [the longest x1 43.2 us: per_device(): pl.pallas_call(scatter_kernel, out_shape=(jax.ShapeDtypeStruct((reps, slo...]
    dot_general x29 -> x0, matrix products: 83.4 us -> none  [the longest x14 42.4 us: panel_step(): preact = jnp.dot(chosen, flat_weights, preferred_element_type=jnp.float32)]
    reduce_scatter x1 -> x0, waiting for transfers between devices: 41.9 us -> none  [per_device(): lax.psum_scatter(backward.reshape(dpres.shape[1], model_width), 'fsdp', s...]
    gather x30 -> x0, local copies, waits for them, and re-layouts: 41.6 us -> none  [the longest x28 40.1 us: panel_step(): jnp.take(token_blocks, row_ids, axis=1)]
    scatter x1 -> x0, local copies, waits for them, and re-layouts: 36 us -> none  [per_device(): dense_panels = dense_panels.at[slot_ids[:, None], own_rows].set(blocks)]
    dynamic_slice x28 -> x0, local copies, waits for them, and re-layouts: 23.2 us -> none  [per_device(): lax.scan(panel_step, jnp.zeros((), jnp.float32), panel_items)]
    all_to_all x2 -> x0, waiting for transfers between devices: 22.8 us -> none  [the longest x1 22.8 us: per_device(): lax.all_to_all(activations, 'fsdp', split_axis=1, concat_axis=0, tiled=True)]
  transfers between devices with their start and end apart: 5 -> 0, of which waited for: 3 -> 0; matrix products, arithmetic and copies ran while one was open for 8% -> 0% of each run, Pallas kernels for 0% -> 0%
where the time goes in v1:
time: 131 us; the launch traced here: 130 us
  Pallas kernels  121 us (92%)
  other arithmetic  6.78 us (5%)
  local copies, waits for them, and re-layouts  2.17 us (2%)
    pallas_call x1, Pallas kernels, per_device(): pl.pallas_call(scatter_kernel, out_shape=(jax.ShapeDtypeStruct((reps, slo...  43.2 us
    pallas_call x1, Pallas kernels, per_device(): pl.pallas_call(gather_kernel, out_shape=(jax.ShapeDtypeStruct((reps, NF,...  41.1 us
    pallas_call x1, Pallas kernels, per_device(): pl.pallas_call(forward_kernel, out_shape=(jax.ShapeDtypeStruct((NF, slots...  18 us
    pallas_call x1, Pallas kernels, per_device(): pl.pallas_call(functools.partial(weight_kernel, scale), out_shape=jax.Sha...  15.8 us

profile of v1, /device:TPU:0, one launch (start us, length us, event | category | flops | bytes accessed | tf_op | source)
XLA Modules:
  0.0 130.2 jit_solution(7298175416459145350)
XLA Ops:
  0.6 0.8 convert_reduce_fusion.1
  1.4 0.6 fusion.1
  2.0 0.6 add_clamp_fusion.1
  2.7 0.7 select_reduce_fusion
  3.4 1.1 add_subtract_fusion.table
  4.6 0.1 add_clamp_fusion
  4.7 0.7 min.22.table
  5.3 0.1 fusion
  5.4 0.8 reduce_window_sum.11
  6.2 0.3 multiply_reduce_fusion
  6.5 0.3 convert_reduce_fusion
  6.8 0.1 reshape.49
  6.9 1.3 pad_add_fusion.info
  8.2 2.4 %pick_cotangents.1.outgoing = bf16[16,14,16,128]{3,2,1,0:T(8,128)(2,1)} custom-call(s32[224]{0:T(256)} %min.22.table, bf16[16,14336]{1,0:T(8,128)(2,1)} %upstream.1), custom_call_target="tpu_custom_call" | custom-call | tf_op jit(solution)/shard_map/pick_cotangents/pallas_call | solution.py:382
  10.6 41.1 %gather_tokens.1 = (bf16[2,16,16,4096]{3,2,1,0:T(8,128)(2,1)}, bf16[16,14,16,128]{3,2,1,0:T(8,128)(2,1)}) custom-call(bf16[16,4096]{1,0:T(8,128)(2,1)} %tokens.1, bf16[16,14,16,128]{3,2,1,0:T(8,128)(2,1)} %pick_cotangents.1.outgoing), custom_call_target="tpu_custom_call" | custom-call | tf_op jit(solution)/shard_map/gather_tokens/pallas_call | solution.py:390
  51.7 18.0 %forward_panels.1 = (bf16[16,14,16,128]{3,2,1,0:T(8,128)(2,1)}, bf16[14,256,128]{2,1,0:T(8,128)(2,1)}, bf16[16,16,4096]{2,1,0:T(8,128)(2,1)}) custom-call(s32[226]{0:T(256)} %pad_add_fusion.info, bf16[2,16,16,4096]{3,2,1,0:T(8,128)(2,1)} %get-tuple-element.11.tokens, bf16[14,16,128,128]{3,2,1,0:T(8,128)(2,1)} %blocks.1, ...), custom_call_target="tpu_custom_call" | custom-call | tf_op jit(solution)/shard_map/forward_panels/pallas_call | solution.py:404
  69.7 43.2 %scatter_results.1 = (bf16[2,14,256,128]{3,2,1,0:T(8,128)(2,1)}, bf16[16,14336]{1,0:T(8,128)(2,1)}, bf16[16,4096]{1,0:T(8,128)(2,1)}) custom-call(s32[112]{0:T(128)} %add_subtract_fusion.table, bf16[14,256,128]{2,1,0:T(8,128)(2,1)} %get-tuple-element.13.dz, bf16[16,14,16,128]{3,2,1,0:T(8,128)(2,1)} %get-tuple-element.14.act, ...), custom_call_target="tpu_custom_call" | custom-call | tf_op jit(solution)/shard_map/scatter_results/pallas_call | solution.py:433
  112.9 0.0 copy-start
  112.9 0.0 copy-start.1
  112.9 15.8 %weight_panels.1 = bf16[14,16,128,128]{3,2,1,0:T(8,128)(2,1)} custom-call(s32[226]{0:T(256)} %pad_add_fusion.info, bf16[512,4096]{1,0:T(8,128)(2,1)} %bitcast.3, bf16[2,14,256,128]{3,2,1,0:T(8,128)(2,1)} %get-tuple-element.18.dz), custom_call_target="tpu_custom_call" | custom-call | tf_op jit(solution)/shard_map/weight_panels/pallas_call | solution.py:456
  128.7 0.0 copy-done
  128.7 0.8 copy.10
  129.5 0.0 copy-done.1
  129.5 0.7 copy.11
Async XLA Ops:
  112.9 15.9 %copy-start = (bf16[16,14336]{1,0:T(8,128)(2,1)S(1)}, bf16[16,14336]{1,0:T(8,128)(2,1)}, u32[]{:S(2)}) copy-start(bf16[16,14336]{1,0:T(8,128)(2,1)} %get-tuple-element.26) | copy-start | bytes 1376260
  112.9 16.6 %copy-start.1 = (bf16[16,4096]{1,0:T(8,128)(2,1)S(1)}, bf16[16,4096]{1,0:T(8,128)(2,1)}, u32[]{:S(2)}) copy-start(bf16[16,4096]{1,0:T(8,128)(2,1)} %get-tuple-element.27) | copy-start | bytes 393220

commit v2 on v0

v2 whole, which is shorter than its diff:
```python
import functools
import math

import jax
import jax.numpy as jnp
from jax import lax
from jax.experimental import pallas as pl
from jax.experimental.pallas import tpu as pltpu
from jax.sharding import PartitionSpec as P

BF16 = jnp.bfloat16
F32 = jnp.float32
MESH = pl.DeviceIdType.MESH
VMEM_LIMIT = 60 * 1024 * 1024
NZ, NY, NC = 4, 2, 2
NF = NZ * NY * NC


def per_device_general(tokens, upstream, blocks, keep_mask, panel_owner):
    shard_count = lax.axis_size("fsdp")
    own_index = lax.axis_index("fsdp")
    tok_dev = tokens.shape[0]
    model_width = tokens.shape[1]
    slot_count = blocks.shape[0]
    keep_count = blocks.shape[1]
    block_size = blocks.shape[3]
    row_blocks = keep_mask.shape[0]
    panel_count = panel_owner.shape[0]
    group_rows = tok_dev * shard_count
    rep_count = lax.axis_size("rep")
    shard_ids = jnp.arange(shard_count, dtype=jnp.int32)
    member = (panel_owner[:, None] == shard_ids[None, :]).astype(jnp.int32)
    counts = jnp.sum(member, axis=0)
    first_panel = jnp.cumsum(counts) - counts
    slot_ids = jnp.arange(slot_count, dtype=jnp.int32)
    panel_table = jnp.clip(first_panel[:, None] + slot_ids[None, :], 0, panel_count - 1)
    is_mine = shard_ids == own_index
    own_first = jnp.sum(jnp.where(is_mine, first_panel, 0))
    own_count = jnp.sum(jnp.where(is_mine, counts, 0))
    own_live = slot_ids < own_count
    own_panels = jnp.clip(own_first + slot_ids, 0, panel_count - 1)
    panel_ids = jnp.arange(panel_count, dtype=jnp.int32)
    panel_pick = (panel_ids[None, :] == own_panels[:, None]).astype(jnp.int32)
    running = jnp.cumsum(keep_mask, axis=0)
    own_running = jnp.sum(panel_pick[:, None, :] * running[None, :, :], axis=2)
    pick_ids = jnp.arange(keep_count, dtype=jnp.int32)
    own_rows = jnp.sum(
        (own_running[:, :, None] <= pick_ids[None, None, :]).astype(jnp.int32), axis=1
    )
    upstream_panels = jnp.transpose(upstream.reshape(tok_dev, panel_count, block_size), (1, 0, 2))
    outgoing = jnp.take(upstream_panels, panel_table.reshape(-1), axis=0)
    incoming = lax.all_to_all(outgoing, "fsdp", split_axis=0, concat_axis=1, tiled=True)
    group_tokens = lax.all_gather(tokens, "fsdp", axis=0, tiled=True)
    all_tokens = lax.all_gather(group_tokens, "rep", axis=0, tiled=True)
    token_blocks = jnp.transpose(all_tokens).reshape(row_blocks, block_size, rep_count * group_rows)

    dense_panels = jnp.zeros((slot_count, row_blocks, block_size, block_size), blocks.dtype)
    dense_panels = dense_panels.at[slot_ids[:, None], own_rows].set(blocks)
    dense = dense_panels.reshape(slot_count, model_width, block_size)
    preact = lax.dot_general(
        group_tokens, dense, (((1,), (1,)), ((), ())), preferred_element_type=jnp.float32
    )
    sigmoid_z = jax.nn.sigmoid(preact)
    activations = (preact * sigmoid_z).astype(jnp.bfloat16)
    slope = sigmoid_z * (1.0 + preact * (1.0 - sigmoid_z))
    cot = jnp.transpose(incoming, (1, 0, 2)).astype(jnp.float32)
    dpre = jnp.where(own_live[None, :, None], cot * slope, 0.0).astype(jnp.bfloat16)
    dpre_all = lax.all_gather(dpre, "rep", axis=0, tiled=True)
    backward = lax.dot_general(
        dpre, dense, (((1, 2), (0, 2)), ((), ())), preferred_element_type=jnp.float32
    )
    input_grad = lax.psum_scatter(
        backward, "fsdp", scatter_dimension=0, tiled=True
    ).astype(jnp.bfloat16)
    returned = lax.all_to_all(activations, "fsdp", split_axis=0, concat_axis=1, tiled=True)
    panel_first = jnp.sum(member * first_panel[None, :], axis=1)
    panel_slot = panel_owner * slot_count + panel_ids - panel_first
    act_panels = jnp.take(returned, panel_slot, axis=1)
    activation_out = act_panels.reshape(tok_dev, panel_count * block_size)
    scale = 1.0 / math.sqrt(group_rows * rep_count)

    def panel_step(nothing, item):
        row_ids, dz = item
        chosen = jnp.take(token_blocks, row_ids, axis=0)
        grad = lax.dot_general(
            chosen, dz, (((2,), (0,)), ((), ())), preferred_element_type=jnp.float32
        )
        return nothing, (grad * scale).astype(jnp.bfloat16)

    nothing, block_grad = lax.scan(
        panel_step, jnp.zeros((), jnp.float32), (own_rows, jnp.transpose(dpre_all, (1, 0, 2)))
    )
    return (activation_out, input_grad, block_grad)


class Place:
    def __init__(self):
        self.rep = lax.axis_index("rep")
        self.me = lax.axis_index("fsdp")
        self.core = self.me % NC
        self.y = (self.me // NC) % NY
        self.z = self.me // (NC * NY)

    def at(self, z, y, core):
        return (z * NY + y) * NC + core

    def z_back(self, step):
        return (self.z + NZ - step) % NZ

    def z_ahead(self, step):
        return (self.z + step) % NZ

    def fsdp_peer(self, step):
        return (self.me + step) % NF

    def greet(self):
        barrier = pltpu.get_barrier_semaphore()
        for step in range(1, NF):
            pl.semaphore_signal(
                barrier, inc=1, device_id=(self.rep, self.fsdp_peer(step)), device_id_type=MESH
            )
        pl.semaphore_signal(barrier, inc=1, device_id=(1 - self.rep, self.me), device_id_type=MESH)
        pl.semaphore_wait(barrier, NF)


def send(src, dst, sems, slot, device):
    send_sems, recv_sems = sems
    copy = pltpu.make_async_remote_copy(
        src_ref=src,
        dst_ref=dst,
        send_sem=send_sems.at[slot],
        recv_sem=recv_sems.at[slot],
        device_id=device,
        device_id_type=MESH,
    )
    copy.start()
    return copy


def layer_kernel(
    scale,
    first, owner, keep, tokens, upstream, blocks_hbm,
    act_out, grad_out, block_grad,
    all_tokens, turned, dense, blocks, grads, up3, outgoing, incoming,
    act, act_in, dz_both, dz_flat, part, r1, s2, r2, s3, r3, run, place_of, kept_row,
    local, z_s, z_r, y_s, y_r, x_s, x_r, d_s, d_r, c_s, c_r, u_s, u_r,
    v_s, v_r, a_s, a_r, p_s, p_r, q_s, q_r, t_s, t_r,
):
    place = Place()
    rep, me, z, y, core = place.rep, place.me, place.z, place.y, place.core
    slots, bs = outgoing.shape[1], outgoing.shape[3]
    row_blocks, panels = keep.shape
    kept = block_grad.shape[1]
    tok_dev, width = tokens.shape
    rows = NF * tok_dev
    pairs = slots // 2
    y_peer = (rep, place.at(z, 1 - y, core))
    x_peer = (1 - rep, me)
    core_peer = (rep, place.at(z, y, 1 - core))
    z_sems, y_sems, x_sems = (z_s, z_r), (y_s, y_r), (x_s, x_r)
    d_sems, c_sems, u_sems = (d_s, d_r), (c_s, c_r), (u_s, u_r)
    early = pairs // 2 + 1
    halves = ((0, 2 * early), (2 * early, slots - 2 * early))

    load_blocks = pltpu.make_async_copy(
        blocks_hbm, blocks.at[pl.ds(0, slots * kept)], local.at[0]
    )
    load_blocks.start()
    all_tokens[rep, me] = tokens[...]
    place.greet()

    own = all_tokens.at[rep, me]
    z_copies = {}
    for step in range(1, NZ):
        peer = (rep, place.at(place.z_ahead(step), y, core))
        z_copies[step] = send(own, own, z_sems, step - 1, peer)
    y_copies, x_copies, d_copies, c_copies = [], [], [None] * NZ, [None] * (4 * NZ)

    def spread(step):
        piece = all_tokens.at[rep, place.at(place.z_back(step), y, core)]
        y_copies.append(send(piece, piece, y_sems, step, y_peer))
        x_copies.append(send(piece, piece, x_sems, step, x_peer))
        c_copies[step] = send(piece, piece, c_sems, step, core_peer)

    spread(0)

    for c in range(panels):
        up3[c] = upstream[:, c * bs:(c + 1) * bs]
    u_copies = [[], []]
    for half, (start, size) in enumerate(halves):
        @pl.loop(0, NF)
        def _(k):
            for p in range(start, start + size):
                outgoing[k, p] = up3[jnp.minimum(first[k] + p, panels - 1)]

        for step in range(1, NF):
            peer = place.fsdp_peer(step)
            span = pl.ds(start, size)
            u_copies[half].append(send(
                outgoing.at[peer, span], incoming.at[me, span], u_sems,
                half * (NF - 1) + step - 1, (rep, peer),
            ))
    incoming[me] = outgoing[me]

    @pl.loop(0, slots)
    def _(p):
        c = jnp.minimum(first[me] + p, panels - 1)
        count = jnp.int32(0)
        for r in range(row_blocks):
            bit = keep[r, c]
            count = count + bit
            run[p * row_blocks + r] = count
            place_of[p * row_blocks + r] = jnp.where(
                bit == 1, p * kept + jnp.clip(count - 1, 0, kept - 1), slots * kept
            )

    blocks[slots * kept] = jnp.zeros((bs, bs), BF16)
    load_blocks.wait()

    def build(start, stop):
        @pl.loop(start, stop)
        def _(i):
            for side in range(2):
                for r in range(row_blocks):
                    at = place_of[(2 * i + side) * row_blocks + r]
                    dense[i, r * bs:(r + 1) * bs, side * bs:(side + 1) * bs] = blocks[at]

    for step in range(1, NZ):
        z_copies[step].wait_recv()
        spread(step)
        build(step - 1, step)
    for step in range(NZ):
        f_x = place.at(place.z_back(step), y, core)
        f_y = place.at(place.z_back(step), 1 - y, core)
        y_copies[step].wait_recv()
        piece = all_tokens.at[rep, f_y]
        c_copies[2 * NZ + step] = send(piece, piece, c_sems, 2 * NZ + step, core_peer)
        if step % 2 == 1:
            d_copies[step] = send(piece, piece, d_sems, step, x_peer)
        x_copies[step].wait_recv()
        piece = all_tokens.at[1 - rep, f_x]
        if step % 2 == 0:
            d_copies[step] = send(piece, piece, d_sems, step, y_peer)
        c_copies[NZ + step] = send(piece, piece, c_sems, NZ + step, core_peer)
        build(NZ - 1 + step, NZ + step)

    @pl.loop(0, slots)
    def _(p):
        @pl.loop(0, kept)
        def _(j):
            row = jnp.int32(0)
            for r in range(row_blocks):
                row = row + jnp.where(run[p * row_blocks + r] <= j, 1, 0)
            kept_row[p * kept + j] = jnp.minimum(row, row_blocks - 1)

    for step in range(NZ):
        c_copies[step].wait_recv()
        c_copies[2 * NZ + step].wait_recv()

    count = first[me + 1] - first[me]
    v_copies, a_copies = [], []
    for half, (start, size) in enumerate(halves):
        for copy in u_copies[half]:
            copy.wait_recv()

        @pl.loop(start // 2, (start + size) // 2)
        def _(i):
            preact = jnp.dot(
                all_tokens[rep].reshape(rows, width), dense[i], preferred_element_type=F32
            )
            for side in range(2):
                slot = 2 * i + side
                zed = preact[:, side * bs:(side + 1) * bs]
                sig = jax.nn.sigmoid(zed)
                act[:, slot] = (zed * sig).astype(BF16).reshape(NF, tok_dev, bs)
                slope = sig * (1.0 + zed * (1.0 - sig))
                cot = incoming[:, slot].reshape(rows, bs).astype(F32)
                value = jnp.where(slot < count, cot * slope, 0.0).astype(BF16)
                dz_both[rep, slot] = value
                dz_flat[i, :, side * bs:(side + 1) * bs] = value

        span = pl.ds(start, size)
        piece = dz_both.at[rep, span]
        v_copies.append(send(piece, piece, (v_s, v_r), half, x_peer))
        for step in range(1, NF):
            peer = place.fsdp_peer(step)
            a_copies.append(send(
                act.at[peer, span], act_in.at[pl.ds(me * slots + start, size)], (a_s, a_r),
                half * (NF - 1) + step - 1, (rep, peer),
            ))
        if half == 0:
            for step in range(NZ):
                d_copies[step].wait_recv()
                piece = all_tokens.at[1 - rep, place.at(place.z_back(step), 1 - y, core)]
                c_copies[3 * NZ + step] = send(piece, piece, c_sems, 3 * NZ + step, core_peer)
    act_in[pl.ds(me * slots, slots)] = act[me]

    chunks = 4
    chunk = width // chunks
    p_copies, q_copies, t_copies = [], [], []
    for n in range(chunks):
        span = pl.ds(n * chunk, chunk)
        total = jnp.zeros((rows, chunk), F32)
        for i in range(pairs):
            total = total + lax.dot_general(
                dz_flat[i], dense[i, span, :], (((1,), (1,)), ((), ())),
                preferred_element_type=F32,
            )
        part[:, :, :, :, span] = total.astype(BF16).reshape(NZ, NY, NC, tok_dev, chunk)
        p_copies.append(send(
            part.at[:, :, 1 - core, :, span], r1.at[:, :, :, span], (p_s, p_r), n, core_peer
        ))
    for n in range(chunks):
        span = pl.ds(n * chunk, chunk)
        p_copies[n].wait_recv()
        s2[:, :, span] = (
            part[:, 1 - y, core, :, span].astype(F32) + r1[:, 1 - y, :, span].astype(F32)
        ).astype(BF16)
        q_copies.append(send(s2.at[:, :, span], r2.at[:, :, span], (q_s, q_r), n, y_peer))

    def column_sum(at_z, span):
        return (
            part[at_z, y, core, :, span].astype(F32)
            + r1[at_z, y, :, span].astype(F32)
            + r2[at_z, :, span].astype(F32)
        )

    def to_z(n):
        span = pl.ds(n * chunk, chunk)
        q_copies[n].wait_recv()
        for step in range(1, NZ):
            s3[step - 1, :, span] = column_sum(place.z_ahead(step), span).astype(BF16)
            peer = (rep, place.at(place.z_ahead(step), y, core))
            t_copies.append(send(
                s3.at[step - 1, :, span], r3.at[step - 1, :, span], (t_s, t_r),
                n * (NZ - 1) + step - 1, peer,
            ))

    stores = []

    def weight(start, size):
        @pl.loop(start, start + size)
        def _(p):
            value = dz_both[:, p].reshape(2 * rows, bs)
            for j in range(kept):
                grads[p, j] = (
                    jnp.dot(
                        turned[kept_row[p * kept + j]], value, preferred_element_type=F32
                    ) * scale
                ).astype(BF16)

        span = pl.ds(start, size)
        stores.append(pltpu.make_async_copy(
            grads.at[span], block_grad.at[span], local.at[1 + len(stores)]
        ))
        stores[-1].start()

    for step in range(NZ):
        c_copies[NZ + step].wait_recv()
        c_copies[3 * NZ + step].wait_recv()

    @pl.loop(0, row_blocks)
    def _(r):
        lanes = pl.ds(pl.multiple_of(r * bs, bs), bs)
        turned[r] = all_tokens[:, :, :, lanes].reshape(2 * rows, bs).T

    v_copies[0].wait_recv()
    cut = halves[0][1] // 2
    to_z(0)
    weight(0, cut)
    to_z(1)
    to_z(2)
    weight(cut, halves[0][1] - cut)
    to_z(3)
    v_copies[1].wait_recv()
    weight(*halves[1])
    for n in range(chunks):
        span = pl.ds(n * chunk, chunk)
        total = column_sum(z, span)
        for step in range(1, NZ):
            t_copies[n * (NZ - 1) + step - 1].wait_recv()
            total = total + r3[step - 1, :, span].astype(F32)
        grad_out[:, span] = total.astype(BF16)
    for copy in a_copies:
        copy.wait_recv()

    @pl.loop(0, panels)
    def _(c):
        k = owner[c]
        at = jnp.clip(k * slots + c - first[k], 0, NF * slots - 1)
        act_out[:, pl.ds(pl.multiple_of(c * bs, bs), bs)] = act_in[at]

    for store in stores:
        store.wait()
    sent = list(z_copies.values()) + y_copies + x_copies + d_copies + c_copies + u_copies[0]
    sent += u_copies[1] + v_copies + a_copies + p_copies + q_copies + t_copies
    for copy in sent:
        copy.wait_send()


def per_device(tokens, upstream, blocks, keep_mask, panel_owner):
    tok_dev, width = tokens.shape
    slots, keep, bs, _ = blocks.shape
    panels = panel_owner.shape[0]
    row_blocks = keep_mask.shape[0]
    reps = 2
    group = NF * tok_dev
    pairs = slots // 2
    shard_ids = jnp.arange(NF + 1, dtype=jnp.int32)
    below = (panel_owner[:, None] < shard_ids[None, :]).astype(jnp.int32)
    first = jnp.sum(below, axis=0)

    smem = pl.BlockSpec(memory_space=pltpu.SMEM)
    vmem = pl.BlockSpec(memory_space=pltpu.VMEM)
    anywhere = pl.BlockSpec(memory_space=pl.ANY)
    dma = lambda n: [pltpu.SemaphoreType.DMA((n,))] * 2
    act_out, input_grad, block_grad = pl.pallas_call(
        functools.partial(layer_kernel, 1.0 / math.sqrt(group * reps)),
        out_shape=(
            jax.ShapeDtypeStruct((tok_dev, panels * bs), BF16),
            jax.ShapeDtypeStruct((tok_dev, width), BF16),
            jax.ShapeDtypeStruct((slots, keep, bs, bs), BF16),
        ),
        in_specs=[smem, smem, smem, vmem, vmem, anywhere],
        out_specs=(vmem, vmem, anywhere),
        scratch_shapes=[
            pltpu.VMEM((reps, NF, tok_dev, width), BF16),
            pltpu.VMEM((row_blocks, bs, reps * group), BF16),
            pltpu.VMEM((pairs, width, 2 * bs), BF16),
            pltpu.VMEM((slots * keep + 1, bs, bs), BF16),
            pltpu.VMEM((slots, keep, bs, bs), BF16),
            pltpu.VMEM((panels, tok_dev, bs), BF16),
            pltpu.VMEM((NF, slots, tok_dev, bs), BF16),
            pltpu.VMEM((NF, slots, tok_dev, bs), BF16),
            pltpu.VMEM((NF, slots, tok_dev, bs), BF16),
            pltpu.VMEM((NF * slots, tok_dev, bs), BF16),
            pltpu.VMEM((reps, slots, group, bs), BF16),
            pltpu.VMEM((pairs, group, 2 * bs), BF16),
            pltpu.VMEM((NZ, NY, NC, tok_dev, width), BF16),
            pltpu.VMEM((NZ, NY, tok_dev, width), BF16),
            pltpu.VMEM((NZ, tok_dev, width), BF16),
            pltpu.VMEM((NZ, tok_dev, width), BF16),
            pltpu.VMEM((NZ - 1, tok_dev, width), BF16),
            pltpu.VMEM((NZ - 1, tok_dev, width), BF16),
            pltpu.SMEM((slots * row_blocks,), jnp.int32),
            pltpu.SMEM((slots * row_blocks,), jnp.int32),
            pltpu.SMEM((slots * keep,), jnp.int32),
            pltpu.SemaphoreType.DMA((8,)),
        ]
        + dma(NZ - 1) + dma(NZ) + dma(NZ) + dma(NZ) + dma(4 * NZ) + dma(2 * (NF - 1))
        + dma(2) + dma(2 * (NF - 1)) + dma(4) + dma(4) + dma(4 * (NZ - 1)),
        compiler_params=pltpu.CompilerParams(
            collective_id=0, has_side_effects=True, vmem_limit_bytes=VMEM_LIMIT
        ),
        name="layer",
    )(first, panel_owner, keep_mask, tokens, upstream, blocks.reshape(slots * keep, bs, bs))
    return (act_out, input_grad, block_grad)


def solution(mesh):
    fits = mesh.shape["rep"] == 2 and mesh.shape["fsdp"] == NF
    return jax.shard_map(
        per_device if fits else per_device_general,
        mesh=mesh,
        in_specs=(
            P(("rep", "fsdp"), None),
            P(("rep", "fsdp"), None),
            P("fsdp", None, None, None),
            P(),
            P(),
        ),
        out_specs=(P(("rep", "fsdp"), None), P(("rep", "fsdp"), None), P("fsdp", None, None, None)),
        check_vma=False,
    )
```

time: 687 us -> 96.9 us (0.14)
  the two profiles are of different devices: /device:TPU:0 before, /device:TPU:28 now
where the time goes in v2:
time: 96.9 us; the launch traced here: 96.7 us
  Pallas kernels  82 us (85%)
  local copies, waits for them, and re-layouts  12.7 us (13%)
  other arithmetic  1.28 us (1%)
    pallas_call x1, Pallas kernels, per_device(): pl.pallas_call(functools.partial(layer_kernel, 1.0 / math.sqrt(group * re...  82 us
    unnamed x3, local copies, waits for them, and re-layouts  12.7 us

profile of v2, /device:TPU:28, one launch (start us, length us, event | category | flops | bytes accessed | tf_op | source)
XLA Modules:
  0.0 96.7 jit_solution(16784528128002816191)
XLA Ops:
  0.6 1.3 %convert_reduce_fusion.first = s32[17]{0:T(128)} fusion(s32[112]{0:T(128)} %owner.1), kind=kLoop, calls=%fused_computation | loop fusion | flops 5695 | bytes 516 | tf_op jit(solution)/shard_map/reduce_sum | solution.py:411
  1.9 82.0 %layer.1 = (bf16[16,14336]{1,0:T(8,128)(2,1)}, bf16[16,4096]{1,0:T(8,128)(2,1)}, bf16[14,16,128,128]{3,2,1,0:T(8,128)(2,1)}) custom-call(s32[17]{0:T(128)} %convert_reduce_fusion.first, s32[112]{0:T(128)} %owner.1, s32[32,112]{1,0:T(8,128)} %keep.1, bf16[16,4096]{1,0:T(8,128)(2,1)} %tokens.1, bf16[16,14336]{1,0:T(8,128)(2,1)} %upstream.1, ...), custom_call_target="tpu_custom_call" | custom-call | tf_op jit(solution)/shard_map/layer/pallas_call | solution.py:417
  83.9 1.8 %copy.11 = bf16[16,14336]{1,0:T(8,128)(2,1)} copy(bf16[16,14336]{1,0:T(8,128)(2,1)} %get-tuple-element.6) | data formatting | bytes 917504
  85.8 1.6 %copy.12 = bf16[16,4096]{1,0:T(8,128)(2,1)} copy(bf16[16,4096]{1,0:T(8,128)(2,1)} %get-tuple-element.7) | data formatting | bytes 262144
  87.3 9.3 %copy.13 = bf16[14,16,128,128]{3,2,1,0:T(8,128)(2,1)} copy(bf16[14,16,128,128]{3,2,1,0:T(8,128)(2,1)} %get-tuple-element.8) | data formatting | bytes 14680064

commit v3 on v2

--- a/solution.py
+++ b/solution.py
@@ -139,10 +139,10 @@
 
 def layer_kernel(
     scale,
-    first, owner, keep, tokens, upstream, blocks_hbm,
-    act_out, grad_out, block_grad,
+    first, keep, tokens, upstream, blocks_hbm,
+    act_in, grad_out, early_grads, turned_out, dz_late, kept_row,
     all_tokens, turned, dense, blocks, grads, up3, outgoing, incoming,
-    act, act_in, dz_both, dz_flat, part, r1, s2, r2, s3, r3, run, place_of, kept_row,
+    act, slope, dz_both, dz_flat, part, r1, s2, r2, s3, r3, run, place_of,
     local, z_s, z_r, y_s, y_r, x_s, x_r, d_s, d_r, c_s, c_r, u_s, u_r,
     v_s, v_r, a_s, a_r, p_s, p_r, q_s, q_r, t_s, t_r,
 ):
@@ -150,7 +150,7 @@
     rep, me, z, y, core = place.rep, place.me, place.z, place.y, place.core
     slots, bs = outgoing.shape[1], outgoing.shape[3]
     row_blocks, panels = keep.shape
-    kept = block_grad.shape[1]
+    kept = early_grads.shape[1]
     tok_dev, width = tokens.shape
     rows = NF * tok_dev
     pairs = slots // 2
@@ -260,9 +260,6 @@
     count = first[me + 1] - first[me]
     v_copies, a_copies = [], []
     for half, (start, size) in enumerate(halves):
-        for copy in u_copies[half]:
-            copy.wait_recv()
-
         @pl.loop(start // 2, (start + size) // 2)
         def _(i):
             preact = jnp.dot(
@@ -273,15 +270,9 @@
                 zed = preact[:, side * bs:(side + 1) * bs]
                 sig = jax.nn.sigmoid(zed)
                 act[:, slot] = (zed * sig).astype(BF16).reshape(NF, tok_dev, bs)
-                slope = sig * (1.0 + zed * (1.0 - sig))
-                cot = incoming[:, slot].reshape(rows, bs).astype(F32)
-                value = jnp.where(slot < count, cot * slope, 0.0).astype(BF16)
-                dz_both[rep, slot] = value
-                dz_flat[i, :, side * bs:(side + 1) * bs] = value
+                slope[slot] = sig * (1.0 + zed * (1.0 - sig))
 
         span = pl.ds(start, size)
-        piece = dz_both.at[rep, span]
-        v_copies.append(send(piece, piece, (v_s, v_r), half, x_peer))
         for step in range(1, NF):
             peer = place.fsdp_peer(step)
             a_copies.append(send(
@@ -294,6 +285,30 @@
                 piece = all_tokens.at[1 - rep, place.at(place.z_back(step), 1 - y, core)]
                 c_copies[3 * NZ + step] = send(piece, piece, c_sems, 3 * NZ + step, core_peer)
     act_in[pl.ds(me * slots, slots)] = act[me]
+
+    def turn(group):
+        @pl.loop(0, row_blocks)
+        def _(r):
+            lanes = pl.ds(pl.multiple_of(r * bs, bs), bs)
+            span = pl.ds(pl.multiple_of(group * rows, rows), rows)
+            turned[r, :, span] = all_tokens[group, :, :, lanes].reshape(rows, bs).T
+
+    turn(rep)
+    for half, (start, size) in enumerate(halves):
+        for copy in u_copies[half]:
+            copy.wait_recv()
+
+        @pl.loop(start // 2, (start + size) // 2)
+        def _(i):
+            for side in range(2):
+                slot = 2 * i + side
+                cot = incoming[:, slot].reshape(rows, bs).astype(F32)
+                value = jnp.where(slot < count, cot * slope[slot], 0.0).astype(BF16)
+                dz_both[rep, slot] = value
+                dz_flat[i, :, side * bs:(side + 1) * bs] = value
+
+        piece = dz_both.at[rep, pl.ds(start, size)]
+        v_copies.append(send(piece, piece, (v_s, v_r), half, x_peer))
 
     chunks = 4
     chunk = width // chunks
@@ -338,42 +353,34 @@
 
     stores = []
 
+    def store(src, dst):
+        copy = pltpu.make_async_copy(src, dst, local.at[1 + len(stores)])
+        copy.start()
+        stores.append(copy)
+
     def weight(start, size):
         @pl.loop(start, start + size)
         def _(p):
-            value = dz_both[:, p].reshape(2 * rows, bs)
-            for j in range(kept):
-                grads[p, j] = (
-                    jnp.dot(
-                        turned[kept_row[p * kept + j]], value, preferred_element_type=F32
-                    ) * scale
-                ).astype(BF16)
+            weight_panel(scale, kept_row, p * kept, turned, dz_both[:, p], grads, p)
 
         span = pl.ds(start, size)
-        stores.append(pltpu.make_async_copy(
-            grads.at[span], block_grad.at[span], local.at[1 + len(stores)]
-        ))
-        stores[-1].start()
+        store(grads.at[span], early_grads.at[span])
 
     for step in range(NZ):
         c_copies[NZ + step].wait_recv()
         c_copies[3 * NZ + step].wait_recv()
-
-    @pl.loop(0, row_blocks)
-    def _(r):
-        lanes = pl.ds(pl.multiple_of(r * bs, bs), bs)
-        turned[r] = all_tokens[:, :, :, lanes].reshape(2 * rows, bs).T
-
+    turn(1 - rep)
+    store(turned, turned_out)
+    to_z(0)
+    to_z(1)
     v_copies[0].wait_recv()
     cut = halves[0][1] // 2
-    to_z(0)
     weight(0, cut)
-    to_z(1)
     to_z(2)
+    to_z(3)
     weight(cut, halves[0][1] - cut)
-    to_z(3)
     v_copies[1].wait_recv()
-    weight(*halves[1])
+    store(dz_both.at[:, pl.ds(*halves[1])], dz_late)
     for n in range(chunks):
         span = pl.ds(n * chunk, chunk)
         total = column_sum(z, span)
@@ -383,6 +390,45 @@
         grad_out[:, span] = total.astype(BF16)
     for copy in a_copies:
         copy.wait_recv()
+    for copy in stores:
+        copy.wait()
+    sent = list(z_copies.values()) + y_copies + x_copies + d_copies + c_copies + u_copies[0]
+    sent += u_copies[1] + v_copies + a_copies + p_copies + q_copies + t_copies
+    for copy in sent:
+        copy.wait_send()
+
+
+def weight_panel(scale, kept_row, base, turned, dz, out, at):
+    bs = dz.shape[-1]
+    value = dz.reshape(-1, bs)
+    for j in range(0, out.shape[1], 4):
+        chosen = jnp.concatenate([turned[kept_row[base + j + t]] for t in range(4)], axis=0)
+        grad = jnp.dot(chosen, value, preferred_element_type=F32) * scale
+        out[at, j:j + 4] = grad.astype(BF16).reshape(4, bs, bs)
+
+
+def finish_kernel(
+    scale,
+    first, owner, kept_row, act_in, grad_in, early_grads, turned_hbm, dz_hbm,
+    act_out, grad_out, block_grad,
+    turned, dz, grads, sems,
+):
+    early, kept = early_grads.shape[:2]
+    late = grads.shape[0]
+    slots = early + late
+    bs = turned.shape[1]
+    panels = act_out.shape[1] // bs
+    loads = [
+        pltpu.make_async_copy(dz_hbm, dz, sems.at[0]),
+        pltpu.make_async_copy(turned_hbm, turned, sems.at[1]),
+    ]
+    for copy in loads:
+        copy.start()
+    stores = []
+    for s in range(early):
+        stores.append(pltpu.make_async_copy(early_grads.at[s], block_grad.at[s], sems.at[2 + s]))
+        stores[-1].start()
+    grad_out[...] = grad_in[...]
 
     @pl.loop(0, panels)
     def _(c):
@@ -390,12 +436,16 @@
         at = jnp.clip(k * slots + c - first[k], 0, NF * slots - 1)
         act_out[:, pl.ds(pl.multiple_of(c * bs, bs), bs)] = act_in[at]
 
-    for store in stores:
-        store.wait()
-    sent = list(z_copies.values()) + y_copies + x_copies + d_copies + c_copies + u_copies[0]
-    sent += u_copies[1] + v_copies + a_copies + p_copies + q_copies + t_copies
-    for copy in sent:
-        copy.wait_send()
+    for copy in loads:
+        copy.wait()
+    for s in range(late):
+        weight_panel(scale, kept_row, (early + s) * kept, turned, dz[:, s], grads, s)
+        stores.append(
+            pltpu.make_async_copy(grads.at[s], block_grad.at[early + s], sems.at[2 + early + s])
+        )
+        stores[-1].start()
+    for copy in stores:
+        copy.wait()
 
 
 def per_device(tokens, upstream, blocks, keep_mask, panel_owner):
@@ -414,26 +464,32 @@
     vmem = pl.BlockSpec(memory_space=pltpu.VMEM)
     anywhere = pl.BlockSpec(memory_space=pl.ANY)
     dma = lambda n: [pltpu.SemaphoreType.DMA((n,))] * 2
-    act_out, input_grad, block_grad = pl.pallas_call(
-        functools.partial(layer_kernel, 1.0 / math.sqrt(group * reps)),
+    scale = 1.0 / math.sqrt(group * reps)
+    early = 2 * (pairs // 2 + 1)
+    late = slots - early
+    act_in, grad_in, early_grads, turned, dz_late, kept_row = pl.pallas_call(
+        functools.partial(layer_kernel, scale),
         out_shape=(
-            jax.ShapeDtypeStruct((tok_dev, panels * bs), BF16),
+            jax.ShapeDtypeStruct((NF * slots, tok_dev, bs), BF16),
             jax.ShapeDtypeStruct((tok_dev, width), BF16),
-            jax.ShapeDtypeStruct((slots, keep, bs, bs), BF16),
+            jax.ShapeDtypeStruct((early, keep, bs, bs), BF16),
+            jax.ShapeDtypeStruct((row_blocks, bs, reps * group), BF16),
+            jax.ShapeDtypeStruct((reps, late, group, bs), BF16),
+            jax.ShapeDtypeStruct((slots * keep,), jnp.int32),
         ),
-        in_specs=[smem, smem, smem, vmem, vmem, anywhere],
-        out_specs=(vmem, vmem, anywhere),
+        in_specs=[smem, smem, vmem, vmem, anywhere],
+        out_specs=(vmem, vmem, anywhere, anywhere, anywhere, smem),
         scratch_shapes=[
             pltpu.VMEM((reps, NF, tok_dev, width), BF16),
             pltpu.VMEM((row_blocks, bs, reps * group), BF16),
             pltpu.VMEM((pairs, width, 2 * bs), BF16),
             pltpu.VMEM((slots * keep + 1, bs, bs), BF16),
-            pltpu.VMEM((slots, keep, bs, bs), BF16),
+            pltpu.VMEM((early, keep, bs, bs), BF16),
             pltpu.VMEM((panels, tok_dev, bs), BF16),
             pltpu.VMEM((NF, slots, tok_dev, bs), BF16),
             pltpu.VMEM((NF, slots, tok_dev, bs), BF16),
             pltpu.VMEM((NF, slots, tok_dev, bs), BF16),
-            pltpu.VMEM((NF * slots, tok_dev, bs), BF16),
+            pltpu.VMEM((slots, group, bs), F32),
             pltpu.VMEM((reps, slots, group, bs), BF16),
             pltpu.VMEM((pairs, group, 2 * bs), BF16),
             pltpu.VMEM((NZ, NY, NC, tok_dev, width), BF16),
@@ -444,7 +500,6 @@
             pltpu.VMEM((NZ - 1, tok_dev, width), BF16),
             pltpu.SMEM((slots * row_blocks,), jnp.int32),
             pltpu.SMEM((slots * row_blocks,), jnp.int32),
-            pltpu.SMEM((slots * keep,), jnp.int32),
             pltpu.SemaphoreType.DMA((8,)),
         ]
         + dma(NZ - 1) + dma(NZ) + dma(NZ) + dma(NZ) + dma(4 * NZ) + dma(2 * (NF - 1))
@@ -453,7 +508,25 @@
             collective_id=0, has_side_effects=True, vmem_limit_bytes=VMEM_LIMIT
         ),
         name="layer",
-    )(first, panel_owner, keep_mask, tokens, upstream, blocks.reshape(slots * keep, bs, bs))
+    )(first, keep_mask, tokens, upstream, blocks.reshape(slots * keep, bs, bs))
+    act_out, input_grad, block_grad = pl.pallas_call(
+        functools.partial(finish_kernel, scale),
+        out_shape=(
+            jax.ShapeDtypeStruct((tok_dev, panels * bs), BF16),
+            jax.ShapeDtypeStruct((tok_dev, width), BF16),
+            jax.ShapeDtypeStruct((slots, keep, bs, bs), BF16),
+        ),
+        in_specs=[smem, smem, smem, vmem, vmem, anywhere, anywhere, anywhere],
+        out_specs=(vmem, vmem, anywhere),
+        scratch_shapes=[
+            pltpu.VMEM((row_blocks, bs, reps * group), BF16),
+            pltpu.VMEM((reps, late, group, bs), BF16),
+            pltpu.VMEM((late, keep, bs, bs), BF16),
+            pltpu.SemaphoreType.DMA((2 + slots,)),
+        ],
+        compiler_params=pltpu.CompilerParams(vmem_limit_bytes=VMEM_LIMIT),
+        name="finish",
+    )(first, panel_owner, kept_row, act_in, grad_in, early_grads, turned, dz_late)
     return (act_out, input_grad, block_grad)
 
 

time: 96.9 us -> 213 us (2.20)
  the two profiles are of different devices: /device:TPU:28 before, /device:TPU:0 now
where the time goes in v3:
time: 213 us; the launch traced here: 211 us
  Pallas kernels  208 us (98%)
    pallas_call x1, Pallas kernels, per_device(): pl.pallas_call(functools.partial(finish_kernel, scale), out_shape=(jax.Sh...  130 us
    pallas_call x1, Pallas kernels, per_device(): pl.pallas_call(functools.partial(layer_kernel, scale), out_shape=(jax.Sha...  78.2 us

profile of v3, /device:TPU:0, one launch (start us, length us, event | category | flops | bytes accessed | tf_op | source)
XLA Modules:
  0.0 210.6 jit_solution(2323468665958305966)
XLA Ops:
  0.6 1.3 convert_reduce_fusion.first
  1.9 78.2 %layer.1 = (bf16[224,16,128]{2,1,0:T(8,128)(2,1)}, bf16[16,4096]{1,0:T(8,128)(2,1)}, bf16[8,16,128,128]{3,2,1,0:T(8,128)(2,1)}, bf16[32,128,512]{2,1,0:T(8,128)(...) custom-call(s32[17]{0:T(128)} %convert_reduce_fusion.first, s32[32,112]{1,0:T(8,128)} %keep.1, ...), custom_call_target="tpu_custom_call" | custom-call | tf_op jit(solution)/shard_map/layer/pallas_call | solution.py:470
  80.1 130.3 %finish.1 = (bf16[16,14336]{1,0:T(8,128)(2,1)}, bf16[16,4096]{1,0:T(8,128)(2,1)}, bf16[14,16,128,128]{3,2,1,0:T(8,128)(2,1)}) custom-call(s32[17]{0:T(128)} %convert_reduce_fusion.first, s32[112]{0:T(128)} %owner.1, s32[224]{0:T(256)} %get-tuple-element.9.kept_row, bf16[224,16,128]{2,1,0:T(8,128)(2,1)} %get-tuple-element.10.act_in, ...), custom_call_target="tpu_custom_call" | custom-call | tf_op jit(solution)/shard_map/finish/pallas_call | solution.py:512

commit v4 on v3

--- a/solution.py
+++ b/solution.py
@@ -123,6 +123,17 @@
         pl.semaphore_wait(barrier, NF)
 
 
+def transfer(src, dst, send_sem, recv_sem, device):
+    return pltpu.make_async_remote_copy(
+        src_ref=src,
+        dst_ref=dst,
+        send_sem=send_sem,
+        recv_sem=recv_sem,
+        device_id=device,
+        device_id_type=MESH,
+    )
+
+
 def send(src, dst, sems, slot, device):
     send_sems, recv_sems = sems
     copy = pltpu.make_async_remote_copy(
@@ -142,7 +153,7 @@
     first, keep, tokens, upstream, blocks_hbm,
     act_in, grad_out, early_grads, turned_out, dz_late, kept_row,
     all_tokens, turned, dense, blocks, grads, up3, outgoing, incoming,
-    act, slope, dz_both, dz_flat, part, r1, s2, r2, s3, r3, run, place_of,
+    act, slope, dz_both, dz_flat, part, r1, s2, r2, s3, r3, grad_sum, run, place_of,
     local, z_s, z_r, y_s, y_r, x_s, x_r, d_s, d_r, c_s, c_r, u_s, u_r,
     v_s, v_r, a_s, a_r, p_s, p_r, q_s, q_r, t_s, t_r,
 ):
@@ -157,7 +168,7 @@
     y_peer = (rep, place.at(z, 1 - y, core))
     x_peer = (1 - rep, me)
     core_peer = (rep, place.at(z, y, 1 - core))
-    z_sems, y_sems, x_sems = (z_s, z_r), (y_s, y_r), (x_s, x_r)
+    y_sems, x_sems = (y_s, y_r), (x_s, x_r)
     d_sems, c_sems, u_sems = (d_s, d_r), (c_s, c_r), (u_s, u_r)
     early = pairs // 2 + 1
     halves = ((0, 2 * early), (2 * early, slots - 2 * early))
@@ -169,19 +180,51 @@
     all_tokens[rep, me] = tokens[...]
     place.greet()
 
-    own = all_tokens.at[rep, me]
-    z_copies = {}
-    for step in range(1, NZ):
-        peer = (rep, place.at(place.z_ahead(step), y, core))
-        z_copies[step] = send(own, own, z_sems, step - 1, peer)
+    steps = (
+        0,
+        jnp.where(z == 0, 3, 1),
+        jnp.where((z == 0) | (z == NZ - 1), 2, 3),
+        jnp.where(z == 0, 1, jnp.where(z == NZ - 1, 3, 2)),
+    )
+    up_peer = (rep, place.at(place.z_ahead(1), y, core))
+    down_peer = (rep, place.at(place.z_back(1), y, core))
+
+    def line_piece(n):
+        return all_tokens.at[rep, place.at(place.z_back(steps[n]), y, core)]
+
+    def line_up(n):
+        piece = line_piece(n)
+        return transfer(piece, piece, z_s.at[n], z_r.at[steps[n]], up_peer)
+
+    def line_down(n):
+        piece = line_piece(n)
+        slot = 2 if n == 0 else jnp.maximum(steps[n] - 2, 0)
+        return transfer(piece, piece, z_s.at[NZ + n], z_r.at[slot], down_peer)
+
+    def goes_up(n):
+        return z < NZ - 1 if n == 0 else (z >= steps[n]) & (z < NZ - 1)
+
+    def goes_down(n):
+        return z > 0 if n == 0 else (z < steps[n]) & (z > 0)
+
+    def pass_on(n):
+        @pl.when(goes_up(n))
+        def _():
+            line_up(n).start()
+
+        @pl.when(goes_down(n))
+        def _():
+            line_down(n).start()
+
     y_copies, x_copies, d_copies, c_copies = [], [], [None] * NZ, [None] * (4 * NZ)
 
-    def spread(step):
-        piece = all_tokens.at[rep, place.at(place.z_back(step), y, core)]
-        y_copies.append(send(piece, piece, y_sems, step, y_peer))
-        x_copies.append(send(piece, piece, x_sems, step, x_peer))
-        c_copies[step] = send(piece, piece, c_sems, step, core_peer)
-
+    def spread(n):
+        piece = line_piece(n)
+        y_copies.append(send(piece, piece, y_sems, n, y_peer))
+        x_copies.append(send(piece, piece, x_sems, n, x_peer))
+        c_copies[n] = send(piece, piece, c_sems, n, core_peer)
+
+    pass_on(0)
     spread(0)
 
     for c in range(panels):
@@ -225,24 +268,23 @@
                     at = place_of[(2 * i + side) * row_blocks + r]
                     dense[i, r * bs:(r + 1) * bs, side * bs:(side + 1) * bs] = blocks[at]
 
-    for step in range(1, NZ):
-        z_copies[step].wait_recv()
-        spread(step)
-        build(step - 1, step)
-    for step in range(NZ):
-        f_x = place.at(place.z_back(step), y, core)
-        f_y = place.at(place.z_back(step), 1 - y, core)
-        y_copies[step].wait_recv()
+    for n in range(1, NZ):
+        piece = line_piece(n)
+        transfer(piece, piece, z_s.at[n], z_r.at[steps[n] - 1], up_peer).wait_recv()
+        pass_on(n)
+        spread(n)
+        build(n - 1, n)
+    for n in range(NZ):
+        f_x = place.at(place.z_back(steps[n]), y, core)
+        f_y = place.at(place.z_back(steps[n]), 1 - y, core)
+        y_copies[n].wait_recv()
         piece = all_tokens.at[rep, f_y]
-        c_copies[2 * NZ + step] = send(piece, piece, c_sems, 2 * NZ + step, core_peer)
-        if step % 2 == 1:
-            d_copies[step] = send(piece, piece, d_sems, step, x_peer)
-        x_copies[step].wait_recv()
+        c_copies[2 * NZ + n] = send(piece, piece, c_sems, 2 * NZ + n, core_peer)
+        d_copies[n] = send(piece, piece, d_sems, n, x_peer)
+        x_copies[n].wait_recv()
         piece = all_tokens.at[1 - rep, f_x]
-        if step % 2 == 0:
-            d_copies[step] = send(piece, piece, d_sems, step, y_peer)
-        c_copies[NZ + step] = send(piece, piece, c_sems, NZ + step, core_peer)
-        build(NZ - 1 + step, NZ + step)
+        c_copies[NZ + n] = send(piece, piece, c_sems, NZ + n, core_peer)
+        build(NZ - 1 + n, NZ + n)
 
     @pl.loop(0, slots)
     def _(p):
@@ -282,7 +324,9 @@
         if half == 0:
             for step in range(NZ):
                 d_copies[step].wait_recv()
-                piece = all_tokens.at[1 - rep, place.at(place.z_back(step), 1 - y, core)]
+                piece = all_tokens.at[
+                    1 - rep, place.at(place.z_back(steps[step]), 1 - y, core)
+                ]
                 c_copies[3 * NZ + step] = send(piece, piece, c_sems, 3 * NZ + step, core_peer)
     act_in[pl.ds(me * slots, slots)] = act[me]
 
@@ -312,7 +356,7 @@
 
     chunks = 4
     chunk = width // chunks
-    p_copies, q_copies, t_copies = [], [], []
+    p_copies, q_copies = [], []
     for n in range(chunks):
         span = pl.ds(n * chunk, chunk)
         total = jnp.zeros((rows, chunk), F32)
@@ -340,16 +384,53 @@
             + r2[at_z, :, span].astype(F32)
         )
 
+    def line_sum(n, e, up):
+        span = pl.ds(n * chunk, chunk)
+        way = 0 if up else 1
+        at = (way * chunks + n) * NZ + e
+        return transfer(
+            s3.at[way, e, :, span], r3.at[way, e - 1, :, span], t_s.at[at], t_r.at[at - 1],
+            up_peer if up else down_peer,
+        )
+
+    def line_arrival(n, e, up):
+        span = pl.ds(n * chunk, chunk)
+        way = 0 if up else 1
+        at = (way * chunks + n) * NZ + e
+        return transfer(
+            s3.at[way, e, :, span], r3.at[way, e, :, span], t_s.at[at], t_r.at[at],
+            up_peer if up else down_peer,
+        )
+
+    def ways():
+        for up in (True, False):
+            way = 0 if up else 1
+            has_source = z > 0 if up else z < NZ - 1
+            yield up, way, has_source
+
+    def reaches(e, up):
+        return z + e < NZ if up else z >= e
+
     def to_z(n):
         span = pl.ds(n * chunk, chunk)
         q_copies[n].wait_recv()
-        for step in range(1, NZ):
-            s3[step - 1, :, span] = column_sum(place.z_ahead(step), span).astype(BF16)
-            peer = (rep, place.at(place.z_ahead(step), y, core))
-            t_copies.append(send(
-                s3.at[step - 1, :, span], r3.at[step - 1, :, span], (t_s, t_r),
-                n * (NZ - 1) + step - 1, peer,
-            ))
+        for e in range(NZ - 1, 0, -1):
+            for up, way, has_source in ways():
+                target = z + e if up else z - e
+
+                @pl.when(reaches(e, up) & has_source)
+                def _():
+                    line_arrival(n, e, up).wait_recv()
+                    total = column_sum(target, span) + r3[way, e, :, span].astype(F32)
+                    s3[way, e, :, span] = total.astype(BF16)
+
+                @pl.when(reaches(e, up) & ~has_source)
+                def _():
+                    s3[way, e, :, span] = column_sum(target, span).astype(BF16)
+
+                @pl.when(reaches(e, up))
+                def _():
+                    line_sum(n, e, up).start()
 
     stores = []
 
@@ -383,19 +464,37 @@
     store(dz_both.at[:, pl.ds(*halves[1])], dz_late)
     for n in range(chunks):
         span = pl.ds(n * chunk, chunk)
-        total = column_sum(z, span)
-        for step in range(1, NZ):
-            t_copies[n * (NZ - 1) + step - 1].wait_recv()
-            total = total + r3[step - 1, :, span].astype(F32)
-        grad_out[:, span] = total.astype(BF16)
+        grad_sum[:, span] = column_sum(z, span)
+        for up, way, has_source in ways():
+            @pl.when(has_source)
+            def _():
+                line_arrival(n, 0, up).wait_recv()
+                grad_sum[:, span] += r3[way, 0, :, span].astype(F32)
+
+        grad_out[:, span] = grad_sum[:, span].astype(BF16)
     for copy in a_copies:
         copy.wait_recv()
     for copy in stores:
         copy.wait()
-    sent = list(z_copies.values()) + y_copies + x_copies + d_copies + c_copies + u_copies[0]
-    sent += u_copies[1] + v_copies + a_copies + p_copies + q_copies + t_copies
+    sent = y_copies + x_copies + d_copies + c_copies + u_copies[0]
+    sent += u_copies[1] + v_copies + a_copies + p_copies + q_copies
     for copy in sent:
         copy.wait_send()
+    for n in range(NZ):
+        @pl.when(goes_up(n))
+        def _():
+            line_up(n).wait_send()
+
+        @pl.when(goes_down(n))
+        def _():
+            line_down(n).wait_send()
+
+    for n in range(chunks):
+        for e in range(1, NZ):
+            for up, way, has_source in ways():
+                @pl.when(reaches(e, up))
+                def _():
+                    line_sum(n, e, up).wait_send()
 
 
 def weight_panel(scale, kept_row, base, turned, dz, out, at):
@@ -414,20 +513,17 @@
     turned, dz, grads, sems,
 ):
     early, kept = early_grads.shape[:2]
-    late = grads.shape[0]
-    slots = early + late
+    slots = grads.shape[0]
+    late = slots - early
     bs = turned.shape[1]
     panels = act_out.shape[1] // bs
     loads = [
         pltpu.make_async_copy(dz_hbm, dz, sems.at[0]),
         pltpu.make_async_copy(turned_hbm, turned, sems.at[1]),
+        pltpu.make_async_copy(early_grads, grads.at[pl.ds(0, early)], sems.at[2]),
     ]
     for copy in loads:
         copy.start()
-    stores = []
-    for s in range(early):
-        stores.append(pltpu.make_async_copy(early_grads.at[s], block_grad.at[s], sems.at[2 + s]))
-        stores[-1].start()
     grad_out[...] = grad_in[...]
 
     @pl.loop(0, panels)
@@ -438,10 +534,14 @@
 
     for copy in loads:
         copy.wait()
+    span = pl.ds(0, early)
+    stores = [pltpu.make_async_copy(grads.at[span], block_grad.at[span], sems.at[3])]
+    stores[0].start()
     for s in range(late):
-        weight_panel(scale, kept_row, (early + s) * kept, turned, dz[:, s], grads, s)
+        slot = early + s
+        weight_panel(scale, kept_row, slot * kept, turned, dz[:, s], grads, slot)
         stores.append(
-            pltpu.make_async_copy(grads.at[s], block_grad.at[early + s], sems.at[2 + early + s])
+            pltpu.make_async_copy(grads.at[slot], block_grad.at[slot], sems.at[4 + s])
         )
         stores[-1].start()
     for copy in stores:
@@ -496,14 +596,15 @@
             pltpu.VMEM((NZ, NY, tok_dev, width), BF16),
             pltpu.VMEM((NZ, tok_dev, width), BF16),
             pltpu.VMEM((NZ, tok_dev, width), BF16),
-            pltpu.VMEM((NZ - 1, tok_dev, width), BF16),
-            pltpu.VMEM((NZ - 1, tok_dev, width), BF16),
+            pltpu.VMEM((2, NZ, tok_dev, width), BF16),
+            pltpu.VMEM((2, NZ, tok_dev, width), BF16),
+            pltpu.VMEM((tok_dev, width), F32),
             pltpu.SMEM((slots * row_blocks,), jnp.int32),
             pltpu.SMEM((slots * row_blocks,), jnp.int32),
             pltpu.SemaphoreType.DMA((8,)),
         ]
-        + dma(NZ - 1) + dma(NZ) + dma(NZ) + dma(NZ) + dma(4 * NZ) + dma(2 * (NF - 1))
-        + dma(2) + dma(2 * (NF - 1)) + dma(4) + dma(4) + dma(4 * (NZ - 1)),
+        + dma(2 * NZ) + dma(NZ) + dma(NZ) + dma(NZ) + dma(4 * NZ) + dma(2 * (NF - 1))
+        + dma(2) + dma(2 * (NF - 1)) + dma(4) + dma(4) + dma(2 * 4 * NZ),
         compiler_params=pltpu.CompilerParams(
             collective_id=0, has_side_effects=True, vmem_limit_bytes=VMEM_LIMIT
         ),
@@ -521,8 +622,8 @@
         scratch_shapes=[
             pltpu.VMEM((row_blocks, bs, reps * group), BF16),
             pltpu.VMEM((reps, late, group, bs), BF16),
-            pltpu.VMEM((late, keep, bs, bs), BF16),
-            pltpu.SemaphoreType.DMA((2 + slots,)),
+            pltpu.VMEM((slots, keep, bs, bs), BF16),
+            pltpu.SemaphoreType.DMA((4 + late,)),
         ],
         compiler_params=pltpu.CompilerParams(vmem_limit_bytes=VMEM_LIMIT),
         name="finish",

time: 213 us -> 113 us (0.53); the launches traced: 211 us -> 113 us
  Pallas kernels: 208 us -> 111 us
    pallas_call x1, Pallas kernels: 130 us -> 10 us  [per_device(): pl.pallas_call(functools.partial(finish_kernel, scale), out_shape=(jax.Sh...]
    pallas_call x1, Pallas kernels: 78.2 us -> 101 us  [per_device(): pl.pallas_call(functools.partial(layer_kernel, scale), out_shape=(jax.Sha...]
where the time goes in v4:
time: 113 us
  Pallas kernels  111 us (98%)
  other arithmetic  1.31 us (1%)
    pallas_call x1, Pallas kernels, per_device(): pl.pallas_call(functools.partial(layer_kernel, scale), out_shape=(jax.Sha...  101 us
    pallas_call x1, Pallas kernels, per_device(): pl.pallas_call(functools.partial(finish_kernel, scale), out_shape=(jax.Sh...  10 us

profile of v4, /device:TPU:0, one launch (start us, length us, event | category | flops | bytes accessed | tf_op | source)
XLA Modules:
  0.0 113.2 jit_solution(12779630775143260826)
XLA Ops:
  0.6 1.3 %convert_reduce_fusion.first = s32[17]{0:T(128)} fusion(s32[112]{0:T(128)} %owner.1), kind=kLoop, calls=%fused_computation | loop fusion | flops 5695 | bytes 516 | tf_op jit(solution)/shard_map/reduce_sum | solution.py:561
  1.9 101.1 %layer.1 = (bf16[224,16,128]{2,1,0:T(8,128)(2,1)}, bf16[16,4096]{1,0:T(8,128)(2,1)}, bf16[8,16,128,128]{3,2,1,0:T(8,128)(2,1)}, bf16[32,128,512]{2,1,0:T(8,128)(...) custom-call(s32[17]{0:T(128)} %convert_reduce_fusion.first, s32[32,112]{1,0:T(8,128)} %keep.1, ...), custom_call_target="tpu_custom_call" | custom-call | tf_op jit(solution)/shard_map/layer/pallas_call | solution.py:570
  103.0 10.0 %finish.1 = (bf16[16,14336]{1,0:T(8,128)(2,1)}, bf16[16,4096]{1,0:T(8,128)(2,1)}, bf16[14,16,128,128]{3,2,1,0:T(8,128)(2,1)}) custom-call(s32[17]{0:T(128)} %convert_reduce_fusion.first, s32[112]{0:T(128)} %owner.1, s32[224]{0:T(256)} %get-tuple-element.9.kept_row, bf16[224,16,128]{2,1,0:T(8,128)(2,1)} %get-tuple-element.10.act_in, ...), custom_call_target="tpu_custom_call" | custom-call | tf_op jit(solution)/shard_map/finish/pallas_call | solution.py:613

commit v5 on v3

--- a/solution.py
+++ b/solution.py
@@ -140,9 +140,9 @@
 def layer_kernel(
     scale,
     first, keep, tokens, upstream, blocks_hbm,
-    act_in, grad_out, early_grads, turned_out, dz_late, kept_row,
+    act_in, grad_out, grads_out,
     all_tokens, turned, dense, blocks, grads, up3, outgoing, incoming,
-    act, slope, dz_both, dz_flat, part, r1, s2, r2, s3, r3, run, place_of,
+    act, slope, dz_both, dz_flat, part, r1, s2, r2, s3, r3, run, place_of, kept_row,
     local, z_s, z_r, y_s, y_r, x_s, x_r, d_s, d_r, c_s, c_r, u_s, u_r,
     v_s, v_r, a_s, a_r, p_s, p_r, q_s, q_r, t_s, t_r,
 ):
@@ -150,7 +150,7 @@
     rep, me, z, y, core = place.rep, place.me, place.z, place.y, place.core
     slots, bs = outgoing.shape[1], outgoing.shape[3]
     row_blocks, panels = keep.shape
-    kept = early_grads.shape[1]
+    kept = grads_out.shape[1]
     tok_dev, width = tokens.shape
     rows = NF * tok_dev
     pairs = slots // 2
@@ -187,20 +187,25 @@
     for c in range(panels):
         up3[c] = upstream[:, c * bs:(c + 1) * bs]
     u_copies = [[], []]
-    for half, (start, size) in enumerate(halves):
+
+    def send_cotangents(half):
+        start, size = halves[half]
+
         @pl.loop(0, NF)
         def _(k):
             for p in range(start, start + size):
                 outgoing[k, p] = up3[jnp.minimum(first[k] + p, panels - 1)]
 
+        span = pl.ds(start, size)
+        incoming[me, span] = outgoing[me, span]
         for step in range(1, NF):
             peer = place.fsdp_peer(step)
-            span = pl.ds(start, size)
             u_copies[half].append(send(
                 outgoing.at[peer, span], incoming.at[me, span], u_sems,
                 half * (NF - 1) + step - 1, (rep, peer),
             ))
-    incoming[me] = outgoing[me]
+
+    send_cotangents(0)
 
     @pl.loop(0, slots)
     def _(p):
@@ -229,18 +234,16 @@
         z_copies[step].wait_recv()
         spread(step)
         build(step - 1, step)
+    send_cotangents(1)
     for step in range(NZ):
         f_x = place.at(place.z_back(step), y, core)
         f_y = place.at(place.z_back(step), 1 - y, core)
         y_copies[step].wait_recv()
         piece = all_tokens.at[rep, f_y]
         c_copies[2 * NZ + step] = send(piece, piece, c_sems, 2 * NZ + step, core_peer)
-        if step % 2 == 1:
-            d_copies[step] = send(piece, piece, d_sems, step, x_peer)
+        d_copies[step] = send(piece, piece, d_sems, step, x_peer)
         x_copies[step].wait_recv()
         piece = all_tokens.at[1 - rep, f_x]
-        if step % 2 == 0:
-            d_copies[step] = send(piece, piece, d_sems, step, y_peer)
         c_copies[NZ + step] = send(piece, piece, c_sems, NZ + step, core_peer)
         build(NZ - 1 + step, NZ + step)
 
@@ -272,19 +275,21 @@
                 act[:, slot] = (zed * sig).astype(BF16).reshape(NF, tok_dev, bs)
                 slope[slot] = sig * (1.0 + zed * (1.0 - sig))
 
-        span = pl.ds(start, size)
-        for step in range(1, NF):
-            peer = place.fsdp_peer(step)
-            a_copies.append(send(
-                act.at[peer, span], act_in.at[pl.ds(me * slots + start, size)], (a_s, a_r),
-                half * (NF - 1) + step - 1, (rep, peer),
-            ))
         if half == 0:
             for step in range(NZ):
                 d_copies[step].wait_recv()
                 piece = all_tokens.at[1 - rep, place.at(place.z_back(step), 1 - y, core)]
                 c_copies[3 * NZ + step] = send(piece, piece, c_sems, 3 * NZ + step, core_peer)
     act_in[pl.ds(me * slots, slots)] = act[me]
+
+    def send_activations(half):
+        start, size = halves[half]
+        for step in range(1, NF):
+            peer = place.fsdp_peer(step)
+            a_copies.append(send(
+                act.at[peer, pl.ds(start, size)], act_in.at[pl.ds(me * slots + start, size)],
+                (a_s, a_r), half * (NF - 1) + step - 1, (rep, peer),
+            ))
 
     def turn(group):
         @pl.loop(0, row_blocks)
@@ -309,6 +314,8 @@
 
         piece = dz_both.at[rep, pl.ds(start, size)]
         v_copies.append(send(piece, piece, (v_s, v_r), half, x_peer))
+        if half == 0:
+            send_activations(0)
 
     chunks = 4
     chunk = width // chunks
@@ -332,6 +339,7 @@
             part[:, 1 - y, core, :, span].astype(F32) + r1[:, 1 - y, :, span].astype(F32)
         ).astype(BF16)
         q_copies.append(send(s2.at[:, :, span], r2.at[:, :, span], (q_s, q_r), n, y_peer))
+    send_activations(1)
 
     def column_sum(at_z, span):
         return (
@@ -364,13 +372,12 @@
             weight_panel(scale, kept_row, p * kept, turned, dz_both[:, p], grads, p)
 
         span = pl.ds(start, size)
-        store(grads.at[span], early_grads.at[span])
+        store(grads.at[span], grads_out.at[span])
 
     for step in range(NZ):
         c_copies[NZ + step].wait_recv()
         c_copies[3 * NZ + step].wait_recv()
     turn(1 - rep)
-    store(turned, turned_out)
     to_z(0)
     to_z(1)
     v_copies[0].wait_recv()
@@ -380,7 +387,7 @@
     to_z(3)
     weight(cut, halves[0][1] - cut)
     v_copies[1].wait_recv()
-    store(dz_both.at[:, pl.ds(*halves[1])], dz_late)
+    weight(*halves[1])
     for n in range(chunks):
         span = pl.ds(n * chunk, chunk)
         total = column_sum(z, span)
@@ -408,26 +415,22 @@
 
 
 def finish_kernel(
-    scale,
-    first, owner, kept_row, act_in, grad_in, early_grads, turned_hbm, dz_hbm,
-    act_out, grad_out, block_grad,
-    turned, dz, grads, sems,
+    first, owner, act_in, grad_in, grads_in, act_out, grad_out, block_grad, grads, load, store
 ):
-    early, kept = early_grads.shape[:2]
-    late = grads.shape[0]
-    slots = early + late
-    bs = turned.shape[1]
+    slots = grads.shape[0]
+    bs = act_in.shape[2]
     panels = act_out.shape[1] // bs
     loads = [
-        pltpu.make_async_copy(dz_hbm, dz, sems.at[0]),
-        pltpu.make_async_copy(turned_hbm, turned, sems.at[1]),
+        pltpu.make_async_copy(grads_in.at[s], grads.at[s], load.at[s]) for s in range(slots)
+    ]
+    stores = [
+        pltpu.make_async_copy(grads.at[s], block_grad.at[s], store.at[s]) for s in range(slots)
     ]
     for copy in loads:
         copy.start()
-    stores = []
-    for s in range(early):
-        stores.append(pltpu.make_async_copy(early_grads.at[s], block_grad.at[s], sems.at[2 + s]))
-        stores[-1].start()
+    for s in range(slots // 2):
+        loads[s].wait()
+        stores[s].start()
     grad_out[...] = grad_in[...]
 
     @pl.loop(0, panels)
@@ -436,14 +439,9 @@
         at = jnp.clip(k * slots + c - first[k], 0, NF * slots - 1)
         act_out[:, pl.ds(pl.multiple_of(c * bs, bs), bs)] = act_in[at]
 
-    for copy in loads:
-        copy.wait()
-    for s in range(late):
-        weight_panel(scale, kept_row, (early + s) * kept, turned, dz[:, s], grads, s)
-        stores.append(
-            pltpu.make_async_copy(grads.at[s], block_grad.at[early + s], sems.at[2 + early + s])
-        )
-        stores[-1].start()
+    for s in range(slots // 2, slots):
+        loads[s].wait()
+        stores[s].start()
     for copy in stores:
         copy.wait()
 
@@ -465,26 +463,21 @@
     anywhere = pl.BlockSpec(memory_space=pl.ANY)
     dma = lambda n: [pltpu.SemaphoreType.DMA((n,))] * 2
     scale = 1.0 / math.sqrt(group * reps)
-    early = 2 * (pairs // 2 + 1)
-    late = slots - early
-    act_in, grad_in, early_grads, turned, dz_late, kept_row = pl.pallas_call(
+    act_in, grad_in, grads = pl.pallas_call(
         functools.partial(layer_kernel, scale),
         out_shape=(
             jax.ShapeDtypeStruct((NF * slots, tok_dev, bs), BF16),
             jax.ShapeDtypeStruct((tok_dev, width), BF16),
-            jax.ShapeDtypeStruct((early, keep, bs, bs), BF16),
-            jax.ShapeDtypeStruct((row_blocks, bs, reps * group), BF16),
-            jax.ShapeDtypeStruct((reps, late, group, bs), BF16),
-            jax.ShapeDtypeStruct((slots * keep,), jnp.int32),
+            jax.ShapeDtypeStruct((slots, keep, bs, bs), BF16),
         ),
         in_specs=[smem, smem, vmem, vmem, anywhere],
-        out_specs=(vmem, vmem, anywhere, anywhere, anywhere, smem),
+        out_specs=(vmem, vmem, anywhere),
         scratch_shapes=[
             pltpu.VMEM((reps, NF, tok_dev, width), BF16),
             pltpu.VMEM((row_blocks, bs, reps * group), BF16),
             pltpu.VMEM((pairs, width, 2 * bs), BF16),
             pltpu.VMEM((slots * keep + 1, bs, bs), BF16),
-            pltpu.VMEM((early, keep, bs, bs), BF16),
+            pltpu.VMEM((slots, keep, bs, bs), BF16),
             pltpu.VMEM((panels, tok_dev, bs), BF16),
             pltpu.VMEM((NF, slots, tok_dev, bs), BF16),
             pltpu.VMEM((NF, slots, tok_dev, bs), BF16),
@@ -500,6 +493,7 @@
             pltpu.VMEM((NZ - 1, tok_dev, width), BF16),
             pltpu.SMEM((slots * row_blocks,), jnp.int32),
             pltpu.SMEM((slots * row_blocks,), jnp.int32),
+            pltpu.SMEM((slots * keep,), jnp.int32),
             pltpu.SemaphoreType.DMA((8,)),
         ]
         + dma(NZ - 1) + dma(NZ) + dma(NZ) + dma(NZ) + dma(4 * NZ) + dma(2 * (NF - 1))
@@ -510,23 +504,22 @@
         name="layer",
     )(first, keep_mask, tokens, upstream, blocks.reshape(slots * keep, bs, bs))
     act_out, input_grad, block_grad = pl.pallas_call(
-        functools.partial(finish_kernel, scale),
+        finish_kernel,
         out_shape=(
             jax.ShapeDtypeStruct((tok_dev, panels * bs), BF16),
             jax.ShapeDtypeStruct((tok_dev, width), BF16),
             jax.ShapeDtypeStruct((slots, keep, bs, bs), BF16),
         ),
-        in_specs=[smem, smem, smem, vmem, vmem, anywhere, anywhere, anywhere],
+        in_specs=[smem, smem, vmem, vmem, anywhere],
         out_specs=(vmem, vmem, anywhere),
         scratch_shapes=[
-            pltpu.VMEM((row_blocks, bs, reps * group), BF16),
-            pltpu.VMEM((reps, late, group, bs), BF16),
-            pltpu.VMEM((late, keep, bs, bs), BF16),
-            pltpu.SemaphoreType.DMA((2 + slots,)),
+            pltpu.VMEM((slots, keep, bs, bs), BF16),
+            pltpu.SemaphoreType.DMA((slots,)),
+            pltpu.SemaphoreType.DMA((slots,)),
         ],
         compiler_params=pltpu.CompilerParams(vmem_limit_bytes=VMEM_LIMIT),
         name="finish",
-    )(first, panel_owner, kept_row, act_in, grad_in, early_grads, turned, dz_late)
+    )(first, panel_owner, act_in, grad_in, grads)
     return (act_out, input_grad, block_grad)
 
 

time: 213 us -> 94 us (0.44)
  Pallas kernels: 208 us -> 91.7 us
    pallas_call x1, Pallas kernels: 130 us -> 7.79 us  [per_device(): pl.pallas_call(finish_kernel, out_shape=(jax.ShapeDtypeStruct((tok_dev, p...]
    pallas_call x1, Pallas kernels: 78.2 us -> 83.9 us  [per_device(): pl.pallas_call(functools.partial(layer_kernel, scale), out_shape=(jax.Sha...]
where the time goes in v5:
time: 94 us; the launch traced here: 93.6 us
  Pallas kernels  91.7 us (98%)
  other arithmetic  1.26 us (1%)
    pallas_call x1, Pallas kernels, per_device(): pl.pallas_call(functools.partial(layer_kernel, scale), out_shape=(jax.Sha...  83.9 us
    pallas_call x1, Pallas kernels, per_device(): pl.pallas_call(finish_kernel, out_shape=(jax.ShapeDtypeStruct((tok_dev, p...  7.79 us

profile of v5, /device:TPU:0, one launch (start us, length us, event | category | flops | bytes accessed | tf_op | source)
XLA Modules:
  0.0 93.6 jit_solution(10761442717801739454)
XLA Ops:
  0.6 1.3 %convert_reduce_fusion.first = s32[17]{0:T(128)} fusion(s32[112]{0:T(128)} %owner.1), kind=kLoop, calls=%fused_computation | loop fusion | flops 5695 | bytes 516 | tf_op jit(solution)/shard_map/reduce_sum | solution.py:459
  1.9 83.9 %layer.1 = (bf16[224,16,128]{2,1,0:T(8,128)(2,1)}, bf16[16,4096]{1,0:T(8,128)(2,1)}, bf16[14,16,128,128]{3,2,1,0:T(8,128)(2,1)}) custom-call(s32[17]{0:T(128)} %convert_reduce_fusion.first, s32[32,112]{1,0:T(8,128)} %keep.1, bf16[16,4096]{1,0:T(8,128)(2,1)} %tokens.1, bf16[16,14336]{1,0:T(8,128)(2,1)} %upstream.1, bf16[224,128,128]{2,1,0:T(8,128)(2,1)} %bitcast.1), custom_call_target="tpu_custom_call" | custom-call | tf_op jit(solution)/shard_map/layer/pallas_call | solution.py:466
  85.8 7.8 %finish.1 = (bf16[16,14336]{1,0:T(8,128)(2,1)}, bf16[16,4096]{1,0:T(8,128)(2,1)}, bf16[14,16,128,128]{3,2,1,0:T(8,128)(2,1)}) custom-call(s32[17]{0:T(128)} %convert_reduce_fusion.first, s32[112]{0:T(128)} %owner.1, bf16[224,16,128]{2,1,0:T(8,128)(2,1)} %get-tuple-element.6.act_in, bf16[16,4096]{1,0:T(8,128)(2,1)} %get-tuple-element.7.grad_in, ...), custom_call_target="tpu_custom_call" | custom-call | tf_op jit(solution)/shard_map/finish/pallas_call | solution.py:506

commit v6 on v5

--- a/solution.py
+++ b/solution.py
@@ -142,9 +142,9 @@
     first, keep, tokens, upstream, blocks_hbm,
     act_in, grad_out, grads_out,
     all_tokens, turned, dense, blocks, grads, up3, outgoing, incoming,
-    act, slope, dz_both, dz_flat, part, r1, s2, r2, s3, r3, run, place_of, kept_row,
+    act, slope, dz_both, dz_flat, part, r1, s2, r2, s3, r3, s4, r4, run, place_of, kept_row,
     local, z_s, z_r, y_s, y_r, x_s, x_r, d_s, d_r, c_s, c_r, u_s, u_r,
-    v_s, v_r, a_s, a_r, p_s, p_r, q_s, q_r, t_s, t_r,
+    v_s, v_r, a_s, a_r, p_s, p_r, q_s, q_r, t_s, t_r, w_s, w_r,
 ):
     place = Place()
     rep, me, z, y, core = place.rep, place.me, place.z, place.y, place.core
@@ -169,15 +169,17 @@
     all_tokens[rep, me] = tokens[...]
     place.greet()
 
+    far = (z + 2) % NZ
+    near = z + 1 - 2 * (z % 2)
+    line = (z, far, near, (near + 2) % NZ)
+    far_peer = (rep, place.at(far, y, core))
+    near_peer = (rep, place.at(near, y, core))
     own = all_tokens.at[rep, me]
-    z_copies = {}
-    for step in range(1, NZ):
-        peer = (rep, place.at(place.z_ahead(step), y, core))
-        z_copies[step] = send(own, own, z_sems, step - 1, peer)
+    z_copies = [send(own, own, z_sems, 0, far_peer), send(own, own, z_sems, 1, near_peer)]
     y_copies, x_copies, d_copies, c_copies = [], [], [None] * NZ, [None] * (4 * NZ)
 
     def spread(step):
-        piece = all_tokens.at[rep, place.at(place.z_back(step), y, core)]
+        piece = all_tokens.at[rep, place.at(line[step], y, core)]
         y_copies.append(send(piece, piece, y_sems, step, y_peer))
         x_copies.append(send(piece, piece, x_sems, step, x_peer))
         c_copies[step] = send(piece, piece, c_sems, step, core_peer)
@@ -188,24 +190,26 @@
         up3[c] = upstream[:, c * bs:(c + 1) * bs]
     u_copies = [[], []]
 
-    def send_cotangents(half):
-        start, size = halves[half]
-
-        @pl.loop(0, NF)
-        def _(k):
-            for p in range(start, start + size):
-                outgoing[k, p] = up3[jnp.minimum(first[k] + p, panels - 1)]
-
-        span = pl.ds(start, size)
-        incoming[me, span] = outgoing[me, span]
+    @pl.loop(0, NF)
+    def _(k):
+        for p in range(slots):
+            outgoing[k, p] = up3[jnp.minimum(first[k] + p, panels - 1)]
+
+    z_copies[0].wait_recv()
+    piece = all_tokens.at[rep, place.at(far, y, core)]
+    z_copies.append(send(piece, piece, z_sems, 2, near_peer))
+    spread(1)
+    z_copies[1].wait_recv()
+    spread(2)
+    for half, (start, size) in enumerate(halves):
         for step in range(1, NF):
             peer = place.fsdp_peer(step)
+            span = pl.ds(start, size)
             u_copies[half].append(send(
                 outgoing.at[peer, span], incoming.at[me, span], u_sems,
                 half * (NF - 1) + step - 1, (rep, peer),
             ))
-
-    send_cotangents(0)
+    incoming[me] = outgoing[me]
 
     @pl.loop(0, slots)
     def _(p):
@@ -230,20 +234,21 @@
                     at = place_of[(2 * i + side) * row_blocks + r]
                     dense[i, r * bs:(r + 1) * bs, side * bs:(side + 1) * bs] = blocks[at]
 
-    for step in range(1, NZ):
-        z_copies[step].wait_recv()
-        spread(step)
-        build(step - 1, step)
-    send_cotangents(1)
+    z_copies[2].wait_recv()
+    spread(3)
+    build(0, NZ - 1)
     for step in range(NZ):
-        f_x = place.at(place.z_back(step), y, core)
-        f_y = place.at(place.z_back(step), 1 - y, core)
+        f_x = place.at(line[step], y, core)
+        f_y = place.at(line[step], 1 - y, core)
         y_copies[step].wait_recv()
         piece = all_tokens.at[rep, f_y]
         c_copies[2 * NZ + step] = send(piece, piece, c_sems, 2 * NZ + step, core_peer)
-        d_copies[step] = send(piece, piece, d_sems, step, x_peer)
+        if step % 2 == 1:
+            d_copies[step] = send(piece, piece, d_sems, step, x_peer)
         x_copies[step].wait_recv()
         piece = all_tokens.at[1 - rep, f_x]
+        if step % 2 == 0:
+            d_copies[step] = send(piece, piece, d_sems, step, y_peer)
         c_copies[NZ + step] = send(piece, piece, c_sems, NZ + step, core_peer)
         build(NZ - 1 + step, NZ + step)
 
@@ -275,21 +280,19 @@
                 act[:, slot] = (zed * sig).astype(BF16).reshape(NF, tok_dev, bs)
                 slope[slot] = sig * (1.0 + zed * (1.0 - sig))
 
+        span = pl.ds(start, size)
+        for step in range(1, NF):
+            peer = place.fsdp_peer(step)
+            a_copies.append(send(
+                act.at[peer, span], act_in.at[pl.ds(me * slots + start, size)], (a_s, a_r),
+                half * (NF - 1) + step - 1, (rep, peer),
+            ))
         if half == 0:
             for step in range(NZ):
                 d_copies[step].wait_recv()
-                piece = all_tokens.at[1 - rep, place.at(place.z_back(step), 1 - y, core)]
+                piece = all_tokens.at[1 - rep, place.at(line[step], 1 - y, core)]
                 c_copies[3 * NZ + step] = send(piece, piece, c_sems, 3 * NZ + step, core_peer)
     act_in[pl.ds(me * slots, slots)] = act[me]
-
-    def send_activations(half):
-        start, size = halves[half]
-        for step in range(1, NF):
-            peer = place.fsdp_peer(step)
-            a_copies.append(send(
-                act.at[peer, pl.ds(start, size)], act_in.at[pl.ds(me * slots + start, size)],
-                (a_s, a_r), half * (NF - 1) + step - 1, (rep, peer),
-            ))
 
     def turn(group):
         @pl.loop(0, row_blocks)
@@ -314,12 +317,10 @@
 
         piece = dz_both.at[rep, pl.ds(start, size)]
         v_copies.append(send(piece, piece, (v_s, v_r), half, x_peer))
-        if half == 0:
-            send_activations(0)
 
     chunks = 4
     chunk = width // chunks
-    p_copies, q_copies, t_copies = [], [], []
+    p_copies, q_copies, t_copies, w_copies = [], [], [], []
     for n in range(chunks):
         span = pl.ds(n * chunk, chunk)
         total = jnp.zeros((rows, chunk), F32)
@@ -339,7 +340,6 @@
             part[:, 1 - y, core, :, span].astype(F32) + r1[:, 1 - y, :, span].astype(F32)
         ).astype(BF16)
         q_copies.append(send(s2.at[:, :, span], r2.at[:, :, span], (q_s, q_r), n, y_peer))
-    send_activations(1)
 
     def column_sum(at_z, span):
         return (
@@ -348,16 +348,18 @@
             + r2[at_z, :, span].astype(F32)
         )
 
-    def to_z(n):
+    def to_near(n):
         span = pl.ds(n * chunk, chunk)
         q_copies[n].wait_recv()
-        for step in range(1, NZ):
-            s3[step - 1, :, span] = column_sum(place.z_ahead(step), span).astype(BF16)
-            peer = (rep, place.at(place.z_ahead(step), y, core))
-            t_copies.append(send(
-                s3.at[step - 1, :, span], r3.at[step - 1, :, span], (t_s, t_r),
-                n * (NZ - 1) + step - 1, peer,
-            ))
+        for t in range(2):
+            s3[t, :, span] = column_sum(line[2 + t], span).astype(BF16)
+        t_copies.append(send(s3.at[:, :, span], r3.at[:, :, span], (t_s, t_r), n, near_peer))
+
+    def to_far(n):
+        span = pl.ds(n * chunk, chunk)
+        t_copies[n].wait_recv()
+        s4[:, span] = (column_sum(far, span) + r3[1, :, span].astype(F32)).astype(BF16)
+        w_copies.append(send(s4.at[:, span], r4.at[:, span], (w_s, w_r), n, far_peer))
 
     stores = []
 
@@ -378,29 +380,27 @@
         c_copies[NZ + step].wait_recv()
         c_copies[3 * NZ + step].wait_recv()
     turn(1 - rep)
-    to_z(0)
-    to_z(1)
+    for n in range(chunks):
+        to_near(n)
     v_copies[0].wait_recv()
     cut = halves[0][1] // 2
     weight(0, cut)
-    to_z(2)
-    to_z(3)
+    for n in range(chunks):
+        to_far(n)
     weight(cut, halves[0][1] - cut)
     v_copies[1].wait_recv()
     weight(*halves[1])
     for n in range(chunks):
         span = pl.ds(n * chunk, chunk)
-        total = column_sum(z, span)
-        for step in range(1, NZ):
-            t_copies[n * (NZ - 1) + step - 1].wait_recv()
-            total = total + r3[step - 1, :, span].astype(F32)
+        w_copies[n].wait_recv()
+        total = column_sum(z, span) + r3[0, :, span].astype(F32) + r4[:, span].astype(F32)
         grad_out[:, span] = total.astype(BF16)
     for copy in a_copies:
         copy.wait_recv()
     for copy in stores:
         copy.wait()
-    sent = list(z_copies.values()) + y_copies + x_copies + d_copies + c_copies + u_copies[0]
-    sent += u_copies[1] + v_copies + a_copies + p_copies + q_copies + t_copies
+    sent = z_copies + y_copies + x_copies + d_copies + c_copies + u_copies[0]
+    sent += u_copies[1] + v_copies + a_copies + p_copies + q_copies + t_copies + w_copies
     for copy in sent:
         copy.wait_send()
 
@@ -489,15 +489,17 @@
             pltpu.VMEM((NZ, NY, tok_dev, width), BF16),
             pltpu.VMEM((NZ, tok_dev, width), BF16),
             pltpu.VMEM((NZ, tok_dev, width), BF16),
-            pltpu.VMEM((NZ - 1, tok_dev, width), BF16),
-            pltpu.VMEM((NZ - 1, tok_dev, width), BF16),
+            pltpu.VMEM((2, tok_dev, width), BF16),
+            pltpu.VMEM((2, tok_dev, width), BF16),
+            pltpu.VMEM((tok_dev, width), BF16),
+            pltpu.VMEM((tok_dev, width), BF16),
             pltpu.SMEM((slots * row_blocks,), jnp.int32),
             pltpu.SMEM((slots * row_blocks,), jnp.int32),
             pltpu.SMEM((slots * keep,), jnp.int32),
             pltpu.SemaphoreType.DMA((8,)),
         ]
         + dma(NZ - 1) + dma(NZ) + dma(NZ) + dma(NZ) + dma(4 * NZ) + dma(2 * (NF - 1))
-        + dma(2) + dma(2 * (NF - 1)) + dma(4) + dma(4) + dma(4 * (NZ - 1)),
+        + dma(2) + dma(2 * (NF - 1)) + dma(4) + dma(4) + dma(4) + dma(4),
         compiler_params=pltpu.CompilerParams(
             collective_id=0, has_side_effects=True, vmem_limit_bytes=VMEM_LIMIT
         ),

time: 94 us -> 98.5 us (1.048)
  Pallas kernels: 91.7 us -> 96.4 us
    pallas_call x1, Pallas kernels: 83.9 us -> 88.6 us  [per_device(): pl.pallas_call(functools.partial(layer_kernel, scale), out_shape=(jax.Sha...]
where the time goes in v6:
time: 98.5 us; the launch traced here: 98.3 us
  Pallas kernels  96.4 us (98%)
  other arithmetic  1.26 us (1%)
    pallas_call x1, Pallas kernels, per_device(): pl.pallas_call(functools.partial(layer_kernel, scale), out_shape=(jax.Sha...  88.6 us
    pallas_call x1, Pallas kernels, per_device(): pl.pallas_call(finish_kernel, out_shape=(jax.ShapeDtypeStruct((tok_dev, p...  7.79 us

profile of v6, /device:TPU:0, one launch (start us, length us, event | category | flops | bytes accessed | tf_op | source)
XLA Modules:
  0.0 98.3 jit_solution(17405589856457982567)
XLA Ops:
  0.6 1.3 %convert_reduce_fusion.first = s32[17]{0:T(128)} fusion(s32[112]{0:T(128)} %owner.1), kind=kLoop, calls=%fused_computation | loop fusion | flops 5695 | bytes 516 | tf_op jit(solution)/shard_map/reduce_sum | solution.py:459
  1.9 88.6 %layer.1 = (bf16[224,16,128]{2,1,0:T(8,128)(2,1)}, bf16[16,4096]{1,0:T(8,128)(2,1)}, bf16[14,16,128,128]{3,2,1,0:T(8,128)(2,1)}) custom-call(s32[17]{0:T(128)} %convert_reduce_fusion.first, s32[32,112]{1,0:T(8,128)} %keep.1, bf16[16,4096]{1,0:T(8,128)(2,1)} %tokens.1, bf16[16,14336]{1,0:T(8,128)(2,1)} %upstream.1, bf16[224,128,128]{2,1,0:T(8,128)(2,1)} %bitcast.1), custom_call_target="tpu_custom_call" | custom-call | tf_op jit(solution)/shard_map/layer/pallas_call | solution.py:466
  90.5 7.8 %finish.1 = (bf16[16,14336]{1,0:T(8,128)(2,1)}, bf16[16,4096]{1,0:T(8,128)(2,1)}, bf16[14,16,128,128]{3,2,1,0:T(8,128)(2,1)}) custom-call(s32[17]{0:T(128)} %convert_reduce_fusion.first, s32[112]{0:T(128)} %owner.1, bf16[224,16,128]{2,1,0:T(8,128)(2,1)} %get-tuple-element.6.act_in, bf16[16,4096]{1,0:T(8,128)(2,1)} %get-tuple-element.7.grad_in, ...), custom_call_target="tpu_custom_call" | custom-call | tf_op jit(solution)/shard_map/finish/pallas_call | solution.py:508

commit v7 on v2

--- a/solution.py
+++ b/solution.py
@@ -139,10 +139,10 @@
 
 def layer_kernel(
     scale,
-    first, owner, keep, tokens, upstream, blocks_hbm,
-    act_out, grad_out, block_grad,
+    first, keep, tokens, upstream, blocks_hbm,
+    act_in, grad_out, block_grad,
     all_tokens, turned, dense, blocks, grads, up3, outgoing, incoming,
-    act, act_in, dz_both, dz_flat, part, r1, s2, r2, s3, r3, run, place_of, kept_row,
+    act, dz_both, dz_flat, part, r1, s2, r2, s3, r3, run, place_of, kept_row,
     local, z_s, z_r, y_s, y_r, x_s, x_r, d_s, d_r, c_s, c_r, u_s, u_r,
     v_s, v_r, a_s, a_r, p_s, p_r, q_s, q_r, t_s, t_r,
 ):
@@ -384,18 +384,44 @@
     for copy in a_copies:
         copy.wait_recv()
 
-    @pl.loop(0, panels)
-    def _(c):
-        k = owner[c]
-        at = jnp.clip(k * slots + c - first[k], 0, NF * slots - 1)
-        act_out[:, pl.ds(pl.multiple_of(c * bs, bs), bs)] = act_in[at]
-
     for store in stores:
         store.wait()
     sent = list(z_copies.values()) + y_copies + x_copies + d_copies + c_copies + u_copies[0]
     sent += u_copies[1] + v_copies + a_copies + p_copies + q_copies + t_copies
     for copy in sent:
         copy.wait_send()
+
+
+def finish_kernel(
+    first, owner, act_in, grad_in, grads_in, act_out, grad_out, block_grad, grads, load, store
+):
+    slots = grads.shape[0]
+    bs = act_in.shape[2]
+    panels = act_out.shape[1] // bs
+    loads = [
+        pltpu.make_async_copy(grads_in.at[s], grads.at[s], load.at[s]) for s in range(slots)
+    ]
+    stores = [
+        pltpu.make_async_copy(grads.at[s], block_grad.at[s], store.at[s]) for s in range(slots)
+    ]
+    for copy in loads:
+        copy.start()
+    for s in range(slots // 2):
+        loads[s].wait()
+        stores[s].start()
+    grad_out[...] = grad_in[...]
+
+    @pl.loop(0, panels)
+    def _(c):
+        k = owner[c]
+        at = jnp.clip(k * slots + c - first[k], 0, NF * slots - 1)
+        act_out[:, pl.ds(pl.multiple_of(c * bs, bs), bs)] = act_in[at]
+
+    for s in range(slots // 2, slots):
+        loads[s].wait()
+        stores[s].start()
+    for copy in stores:
+        copy.wait()
 
 
 def per_device(tokens, upstream, blocks, keep_mask, panel_owner):
@@ -414,14 +440,14 @@
     vmem = pl.BlockSpec(memory_space=pltpu.VMEM)
     anywhere = pl.BlockSpec(memory_space=pl.ANY)
     dma = lambda n: [pltpu.SemaphoreType.DMA((n,))] * 2
-    act_out, input_grad, block_grad = pl.pallas_call(
+    act_in, grad_in, grads = pl.pallas_call(
         functools.partial(layer_kernel, 1.0 / math.sqrt(group * reps)),
         out_shape=(
-            jax.ShapeDtypeStruct((tok_dev, panels * bs), BF16),
+            jax.ShapeDtypeStruct((NF * slots, tok_dev, bs), BF16),
             jax.ShapeDtypeStruct((tok_dev, width), BF16),
             jax.ShapeDtypeStruct((slots, keep, bs, bs), BF16),
         ),
-        in_specs=[smem, smem, smem, vmem, vmem, anywhere],
+        in_specs=[smem, smem, vmem, vmem, anywhere],
         out_specs=(vmem, vmem, anywhere),
         scratch_shapes=[
             pltpu.VMEM((reps, NF, tok_dev, width), BF16),
@@ -433,7 +459,6 @@
             pltpu.VMEM((NF, slots, tok_dev, bs), BF16),
             pltpu.VMEM((NF, slots, tok_dev, bs), BF16),
             pltpu.VMEM((NF, slots, tok_dev, bs), BF16),
-            pltpu.VMEM((NF * slots, tok_dev, bs), BF16),
             pltpu.VMEM((reps, slots, group, bs), BF16),
             pltpu.VMEM((pairs, group, 2 * bs), BF16),
             pltpu.VMEM((NZ, NY, NC, tok_dev, width), BF16),
@@ -453,7 +478,24 @@
             collective_id=0, has_side_effects=True, vmem_limit_bytes=VMEM_LIMIT
         ),
         name="layer",
-    )(first, panel_owner, keep_mask, tokens, upstream, blocks.reshape(slots * keep, bs, bs))
+    )(first, keep_mask, tokens, upstream, blocks.reshape(slots * keep, bs, bs))
+    act_out, input_grad, block_grad = pl.pallas_call(
+        finish_kernel,
+        out_shape=(
+            jax.ShapeDtypeStruct((tok_dev, panels * bs), BF16),
+            jax.ShapeDtypeStruct((tok_dev, width), BF16),
+            jax.ShapeDtypeStruct((slots, keep, bs, bs), BF16),
+        ),
+        in_specs=[smem, smem, vmem, vmem, anywhere],
+        out_specs=(vmem, vmem, anywhere),
+        scratch_shapes=[
+            pltpu.VMEM((slots, keep, bs, bs), BF16),
+            pltpu.SemaphoreType.DMA((slots,)),
+            pltpu.SemaphoreType.DMA((slots,)),
+        ],
+        compiler_params=pltpu.CompilerParams(vmem_limit_bytes=VMEM_LIMIT),
+        name="finish",
+    )(first, panel_owner, act_in, grad_in, grads)
     return (act_out, input_grad, block_grad)
 
 

time: 96.9 us -> 90.6 us (0.935)
  local copies, waits for them, and re-layouts: 12.7 us -> 0 us
  Pallas kernels: 82 us -> 88.6 us
    unnamed x3 -> x0, local copies, waits for them, and re-layouts: 12.7 us -> none
    pallas_call x0 -> x1, Pallas kernels: none -> 7.79 us  [per_device(): pl.pallas_call(finish_kernel, out_shape=(jax.ShapeDtypeStruct((tok_dev, p...]
    pallas_call x1, Pallas kernels: 82 us -> 80.8 us  [per_device(): pl.pallas_call(functools.partial(layer_kernel, 1.0 / math.sqrt(group * re...]
where the time goes in v7:
time: 90.6 us; the launch traced here: 90.5 us
  Pallas kernels  88.6 us (98%)
  other arithmetic  1.26 us (1%)
    pallas_call x1, Pallas kernels, per_device(): pl.pallas_call(functools.partial(layer_kernel, 1.0 / math.sqrt(group * re...  80.8 us
    pallas_call x1, Pallas kernels, per_device(): pl.pallas_call(finish_kernel, out_shape=(jax.ShapeDtypeStruct((tok_dev, p...  7.79 us

profile of v7, /device:TPU:28, one launch (start us, length us, event | category | flops | bytes accessed | tf_op | source)
XLA Modules:
  0.0 90.5 jit_solution(80684619807885226)
XLA Ops:
  0.6 1.3 %convert_reduce_fusion.first = s32[17]{0:T(128)} fusion(s32[112]{0:T(128)} %owner.1), kind=kLoop, calls=%fused_computation | loop fusion | flops 5695 | bytes 516 | tf_op jit(solution)/shard_map/reduce_sum | solution.py:437
  1.9 80.8 %layer.1 = (bf16[224,16,128]{2,1,0:T(8,128)(2,1)}, bf16[16,4096]{1,0:T(8,128)(2,1)}, bf16[14,16,128,128]{3,2,1,0:T(8,128)(2,1)}) custom-call(s32[17]{0:T(128)} %convert_reduce_fusion.first, s32[32,112]{1,0:T(8,128)} %keep.1, bf16[16,4096]{1,0:T(8,128)(2,1)} %tokens.1, bf16[16,14336]{1,0:T(8,128)(2,1)} %upstream.1, bf16[224,128,128]{2,1,0:T(8,128)(2,1)} %bitcast.1), custom_call_target="tpu_custom_call" | custom-call | tf_op jit(solution)/shard_map/layer/pallas_call | solution.py:443
  82.7 7.8 %finish.1 = (bf16[16,14336]{1,0:T(8,128)(2,1)}, bf16[16,4096]{1,0:T(8,128)(2,1)}, bf16[14,16,128,128]{3,2,1,0:T(8,128)(2,1)}) custom-call(s32[17]{0:T(128)} %convert_reduce_fusion.first, s32[112]{0:T(128)} %owner.1, bf16[224,16,128]{2,1,0:T(8,128)(2,1)} %get-tuple-element.6.act_in, bf16[16,4096]{1,0:T(8,128)(2,1)} %get-tuple-element.7.grad_in, ...), custom_call_target="tpu_custom_call" | custom-call | tf_op jit(solution)/shard_map/finish/pallas_call | solution.py:482
